TPU v7x, 32 devices: a whole 2x2x4 slice. The times are simulated.
32 devices in a mesh: dp: 8 (over z, y), tensor: 4 (over x, core).
Axes of the slice: x: 2, y: 2, z: 4, core: 2. Of those that a mesh axis runs over, the one named last changes fastest.
Arguments:
- hidden: bfloat16 [16, 1024, 2048], P('dp', 'tensor'), may hold values from -6 to 6
- pre_gain: float32 [2048], replicated, may hold values from 0.5 to 1.5
- w_zx: bfloat16 [2, 2048, 4096], P(None, 'dp', 'tensor'), may hold values from -0.125 to 0.125
- w_bcdt: bfloat16 [2048, 320], P('dp'), may hold values from -0.125 to 0.125
- conv_x: float32 [5, 4096], P(None, 'tensor'), may hold values from -0.5 to 0.5
- conv_bc: float32 [5, 256], replicated, may hold values from -0.5 to 0.5
- dt_bias: float32 [64], P('tensor'), may hold values from -6 to -2
- a_log: float32 [64], P('tensor'), may hold values from 0 to 2.5
- d_skip: float32 [64], P('tensor'), may hold values from 0.5 to 1.5
- gate_gain: float32 [4096], P('tensor'), may hold values from 0.5 to 1.5
- w_out: bfloat16 [4096, 2048], P('tensor', 'dp'), may hold values from -0.09375 to 0.09375
- cotangent: bfloat16 [16, 1024, 2048], P('dp', 'tensor'), may hold values from -6 to 6
- segments: int32 [16, 1024], P('dp'), may hold values from 0 to 1023, as said below
Outputs:
- out_hidden: bfloat16 [16, 1024, 2048], P('dp', 'tensor')
- d_hidden: float32 [16, 1024, 2048], P('dp', 'tensor')
- d_pre_gain: float32 [2048], replicated
- d_w_zx: float32 [2, 2048, 4096], P(None, 'dp', 'tensor')
- d_w_bcdt: float32 [2048, 320], P('dp')
- d_conv_x: float32 [5, 4096], P(None, 'tensor')
- d_conv_bc: float32 [5, 256], replicated
- d_dt_bias: float32 [64], P('tensor')
- d_a_log: float32 [64], P('tensor')
- d_d_skip: float32 [64], P('tensor')
- d_gate_gain: float32 [4096], P('tensor')
- d_w_out: float32 [4096, 2048], P('tensor', 'dp')
Inputs may be any that keep to these rules, and one draw needn't show every extreme that they name: `segments`: within each sequence a document is numbered by the position of its first token, so numbers never fall along a sequence and the first token has 0; every sequence's last token begins a document of its own, and in every sequence one document covers the positions from 255 to 768.
All inputs are finite; a program needn't handle non-finite values.
Results may differ from a plain program's by a relative error of at most 0.009.
Values may be sent and summed in bfloat16 or wider, within the bound.
A program may use at most 320 MiB of HBM per device.

v0:
```python
from functools import partial

import jax
import jax.numpy as jnp
from jax import lax
from jax.sharding import PartitionSpec as P

BLOCK = 256


EPS = 1e-05
EXACT = lax.Precision.HIGHEST


def rms_scale(values):
    return lax.rsqrt(jnp.mean(values * values, axis=-1, keepdims=True) + EPS)


def causal_conv(values, segment, conv_taps):
    tap_count = conv_taps.shape[0] - 1
    seq_length = values.shape[0]
    outcome = jnp.zeros_like(values) + conv_taps[tap_count]
    for tap_index in range(tap_count):
        lag_steps = tap_count - 1 - tap_index
        earlier_rows = jnp.pad(values, ((lag_steps, 0), (0, 0)))[:seq_length]
        earlier_doc = jnp.pad(segment, (lag_steps, 0), constant_values=-1)[:seq_length]
        outcome = outcome + jnp.where(
            (earlier_doc == segment)[:, None], conv_taps[tap_index] * earlier_rows, 0.0
        )
    return outcome


def state_space(heads_x, step_size, a_log, b_mat, c_mat, segment):
    seq_length, heads, head_dim = heads_x.shape
    blocks = seq_length // BLOCK
    rate = (-jnp.exp(a_log) * step_size).reshape(blocks, BLOCK, heads)
    cumrate = jnp.cumsum(rate, axis=1)
    seg_block = segment.reshape(blocks, BLOCK)
    before = jnp.concatenate([jnp.full((1,), -1, jnp.int32), segment[:-1]]).reshape(blocks, BLOCK)[
        :, 0
    ]
    places = jnp.arange(BLOCK)
    causal = places[:, None] >= places[None, :]
    same_doc = (seg_block[:, :, None] == seg_block[:, None, :]) & causal[None]
    head_cum = jnp.moveaxis(cumrate, 2, 1)
    gaps = head_cum[:, :, :, None] - head_cum[:, :, None, :]
    keeper = same_doc[:, None]
    decay = jnp.where(keeper, jnp.exp(jnp.where(keeper, gaps, 0.0)), 0.0)
    b_blocks = b_mat.reshape(blocks, BLOCK, -1)
    c_blocks = c_mat.reshape(blocks, BLOCK, -1)
    scores = jnp.einsum("cin,cjn->cij", c_blocks, b_blocks, precision=EXACT)
    weighted = (
        heads_x.reshape(blocks, BLOCK, heads, head_dim)
        * step_size.reshape(blocks, BLOCK, heads)[..., None]
    )
    inside = jnp.einsum("chij,cjhp->cihp", decay * scores[:, None], weighted, precision=EXACT)
    last_doc = seg_block == seg_block[:, -1:]
    to_end = jnp.where(last_doc[..., None], jnp.exp(cumrate[:, -1:, :] - cumrate), 0.0)
    block_states = jnp.einsum("cjh,cjhp,cjn->chpn", to_end, weighted, b_blocks, precision=EXACT)
    carry_on = jnp.where((seg_block[:, -1] == before)[:, None], jnp.exp(cumrate[:, -1, :]), 0.0)

    def advance(state, block_pair):
        new_states, factor = block_pair
        return (factor[:, None, None] * state + new_states, state)

    zero_state = jnp.zeros((heads, head_dim, b_mat.shape[1]), jnp.float32)
    _, earlier = lax.scan(advance, zero_state, (block_states, carry_on))
    reads = jnp.where((seg_block == before[:, None])[..., None], jnp.exp(cumrate), 0.0)
    outside = jnp.einsum("cih,cin,chpn->cihp", reads, c_blocks, earlier, precision=EXACT)
    return (inside + outside).reshape(seq_length, heads, head_dim)


def mixer(zx_proj, bc_dt, conv_x, conv_bc, dt_bias, a_log, d_skip, segment, head_first):
    heads = dt_bias.shape[0]
    states = conv_bc.shape[1] // 2
    seq_length = zx_proj.shape[1]
    x_part = jax.nn.silu(causal_conv(zx_proj[1], segment, conv_x))
    bc_part = jax.nn.silu(causal_conv(bc_dt[:, : 2 * states], segment, conv_bc))
    raw_step = lax.dynamic_slice_in_dim(bc_dt, 2 * states + head_first, heads, 1)
    step_size = jax.nn.softplus(raw_step + dt_bias)
    heads_x = x_part.reshape(seq_length, heads, -1)
    mixed = state_space(
        heads_x, step_size, a_log, bc_part[:, :states], bc_part[:, states:], segment
    )
    mixed = mixed + d_skip[None, :, None] * heads_x
    return mixed.reshape(seq_length, -1) * jax.nn.silu(zx_proj[0])


def local(
    hidden,
    pre_gain,
    w_zx,
    w_bcdt,
    conv_x,
    conv_bc,
    dt_bias,
    a_log,
    d_skip,
    gate_gain,
    w_out,
    cotangent,
    segments,
):
    micro = hidden.shape[0]
    piece = hidden.shape[1]
    model_width = hidden.shape[2]
    parts = lax.axis_size("tensor")
    local_heads = dt_bias.shape[0]
    head_first = lax.axis_index("tensor") * local_heads
    row_first = lax.axis_index("tensor") * piece
    inner_width = gate_gain.shape[0] * parts
    grad_zx = jnp.zeros((2, model_width, w_zx.shape[2]), jnp.float32)
    grad_bcdt = jnp.zeros((model_width, w_bcdt.shape[1]), jnp.float32)
    grad_out = jnp.zeros((w_out.shape[0], model_width), jnp.float32)
    grad_conv_x = jnp.zeros_like(conv_x)
    grad_conv_bc = jnp.zeros_like(conv_bc)
    grad_dt_bias = jnp.zeros_like(dt_bias)
    grad_a_log = jnp.zeros_like(a_log)
    grad_d_skip = jnp.zeros_like(d_skip)
    grad_gate = jnp.zeros_like(gate_gain)
    grad_pre = jnp.zeros_like(pre_gain)
    results = []
    input_grads = []
    for micro_index in range(micro):
        gathered = (
            lax.all_gather(w_zx, "dp", axis=1, tiled=True),
            lax.all_gather(w_bcdt, "dp", axis=0, tiled=True),
            lax.all_gather(w_out, "dp", axis=1, tiled=True),
        )
        weight_zx, weight_bcdt, weight_out = gathered
        x_piece = hidden[micro_index].astype(jnp.float32)
        scale_in = rms_scale(x_piece)
        u_piece = (x_piece * scale_in * pre_gain).astype(jnp.bfloat16)
        normed_in, g_full = (
            lax.all_gather(u_piece, "tensor", axis=0, tiled=True),
            lax.all_gather(cotangent[micro_index], "tensor", axis=0, tiled=True),
        )
        zx_proj = jnp.einsum(
            "ld,kde->kle", normed_in, weight_zx, preferred_element_type=jnp.float32
        )
        bc_dt = jnp.dot(normed_in, weight_bcdt, preferred_element_type=jnp.float32)
        segment = segments[micro_index]
        local_fn = partial(mixer, segment=segment, head_first=head_first)
        gated, pullback = jax.vjp(local_fn, zx_proj, bc_dt, conv_x, conv_bc, dt_bias, a_log, d_skip)
        squares = lax.psum(jnp.sum(gated * gated, axis=1), "tensor")
        inverse = lax.rsqrt(squares / inner_width + EPS)[:, None]
        normed_out = (gated * inverse * gate_gain).astype(jnp.bfloat16)
        mixed = lax.psum_scatter(
            jnp.dot(normed_out, weight_out, preferred_element_type=jnp.float32),
            "tensor",
            scatter_dimension=0,
            tiled=True,
        )
        results.append((x_piece + mixed).astype(jnp.bfloat16))
        d_normed = jnp.einsum("ld,ed->le", g_full, weight_out, preferred_element_type=jnp.float32)
        micro_out = jnp.einsum("le,ld->ed", normed_out, g_full, preferred_element_type=jnp.float32)
        grad_gate = grad_gate + jnp.sum(d_normed * gated * inverse, axis=0)
        scaled = d_normed * gate_gain
        inner_dot = lax.psum(jnp.sum(scaled * gated, axis=1), "tensor")
        d_gated = inverse * scaled - gated * inverse**3 * (inner_dot / inner_width)[:, None]
        d_zx, d_bcdt_part, d_conv_x_now, d_conv_bc_now, d_dt_now, d_alog_now, d_skip_now = pullback(
            d_gated
        )
        grad_conv_x = grad_conv_x + d_conv_x_now
        grad_conv_bc = grad_conv_bc + d_conv_bc_now
        grad_dt_bias = grad_dt_bias + d_dt_now
        grad_a_log = grad_a_log + d_alog_now
        grad_d_skip = grad_d_skip + d_skip_now
        d_bcdt_low = lax.psum(d_bcdt_part, "tensor").astype(jnp.bfloat16)
        dzx_low = d_zx.astype(jnp.bfloat16)
        micro_zx = jnp.einsum("ld,kle->kde", normed_in, dzx_low, preferred_element_type=jnp.float32)
        micro_bcdt = jnp.einsum(
            "ld,lc->dc", normed_in, d_bcdt_low, preferred_element_type=jnp.float32
        )
        grad_zx = grad_zx + micro_zx
        grad_bcdt = grad_bcdt + micro_bcdt
        grad_out = grad_out + micro_out
        d_in = lax.psum_scatter(
            jnp.einsum("kle,kde->ld", dzx_low, weight_zx, preferred_element_type=jnp.float32),
            "tensor",
            scatter_dimension=0,
            tiled=True,
        )
        own_rows = lax.dynamic_slice_in_dim(d_bcdt_low, row_first, piece, 0)
        d_in = d_in + jnp.einsum(
            "lc,dc->ld", own_rows, weight_bcdt, preferred_element_type=jnp.float32
        )
        grad_pre = grad_pre + jnp.sum(d_in * x_piece * scale_in, axis=0)
        gain_grad = d_in * pre_gain
        d_x = scale_in * gain_grad - x_piece * scale_in**3 * jnp.mean(
            gain_grad * x_piece, axis=-1, keepdims=True
        )
        input_grads.append(cotangent[micro_index].astype(jnp.float32) + d_x)
    scattered = (
        lax.psum_scatter(grad_zx, "dp", scatter_dimension=1, tiled=True),
        lax.psum_scatter(grad_bcdt, "dp", scatter_dimension=0, tiled=True),
        lax.psum_scatter(grad_out, "dp", scatter_dimension=1, tiled=True),
    )
    small_dp = lax.psum((grad_conv_x, grad_dt_bias, grad_a_log, grad_d_skip, grad_gate), "dp")
    small_all = lax.psum((grad_conv_bc, grad_pre), ("dp", "tensor"))
    return (
        jnp.stack(results),
        jnp.stack(input_grads),
        small_all[1],
        scattered[0],
        scattered[1],
        small_dp[0],
        small_all[0],
        small_dp[1],
        small_dp[2],
        small_dp[3],
        small_dp[4],
        scattered[2],
    )


def solution(mesh):
    placed = (
        P("dp", "tensor", None),
        P(),
        P(None, "dp", "tensor"),
        P("dp", None),
        P(None, "tensor"),
        P(),
        P("tensor"),
        P("tensor"),
        P("tensor"),
        P("tensor"),
        P("tensor", "dp"),
        P("dp", "tensor", None),
        P("dp", None),
    )
    return jax.shard_map(
        local,
        mesh=mesh,
        in_specs=placed,
        out_specs=(
            P("dp", "tensor", None),
            P("dp", "tensor", None),
            P(),
            P(None, "dp", "tensor"),
            P("dp", None),
            P(None, "tensor"),
            P(),
            P("tensor"),
            P("tensor"),
            P("tensor"),
            P("tensor"),
            P("tensor", "dp"),
        ),
        check_vma=False,
    )
```

profile of v0, /device:TPU:0, one launch (start us, length us, event | category | flops | bytes accessed | tf_op | source)
XLA Modules:
  0.0 1675.0 jit_solution(14336082263085344609)
XLA Ops:
  26.5 28.4 %all-gather.14.cloned.1.call-done = bf16[2048,320]{0,1:T(8,128)(2,1)} async-done(((bf16[256,320]{0,1:T(8,128)(2,1)}), bf16[2048,320]{0,1:T(8,128)(2,1)}) %all-gather.14.cloned.1.call-update) | async-done | bytes 1310736 | tf_op jit(solution)/shard_map/all_gather | solution.py:127
  54.9 35.3 %all-gather.18.cloned.1.call-done = bf16[1024,2048]{1,0:T(8,128)(2,1)} async-done(((bf16[256,2048]{1,0:T(8,128)(2,1)}), bf16[1024,2048]{1,0:T(8,128)(2,1)}) %all-gather.18.cloned.1.call-update) | async-done | bytes 4194320 | tf_op jit(solution)/shard_map/all_gather | solution.py:135
  95.6 31.3 %all-gather.10.cloned.1.call-done = bf16[1024,2048]{1,0:T(8,128)(2,1)} async-done(((bf16[256,2048]{1,0:T(8,128)(2,1)}), bf16[1024,2048]{1,0:T(8,128)(2,1)}) %all-gather.10.cloned.1.call-update) | async-done | bytes 4194320 | tf_op jit(solution)/shard_map/all_gather | solution.py:135
  163.9 76.5 %all-gather.16.cloned.1.call-done = bf16[1024,2048]{1,0:T(8,128)(2,1)} async-done(((bf16[1024,256]{1,0:T(8,128)(2,1)}), bf16[1024,2048]{1,0:T(8,128)(2,1)}) %all-gather.16.cloned.1.call-update) | async-done | bytes 4194320 | tf_op jit(solution)/shard_map/all_gather | solution.py:128
  240.4 10.0 fusion.66
  250.4 115.2 %all-gather.12.cloned.1.call-done = bf16[2,2048,1024]{2,1,0:T(8,128)(2,1)} async-done(((bf16[2,256,1024]{2,1,0:T(8,128)(2,1)}), bf16[2,2048,1024]{2,1,0:T(8,128)(2,1)}) %all-gather.12.cloned.1.call-update) | async-done | bytes 8388624 | tf_op jit(solution)/shard_map/all_gather | solution.py:126
  365.6 13.0 fusion.111
  385.3 8.9 fusion.108
  397.5 10.3 fusion.90
  430.7 10.5 while.68
  465.3 13.8 while.69
  484.9 20.4 %fusion.81 = f32[4,256,16,64]{1,3,2,0:T(8,128)} fusion(f32[4,16,64,256]{3,2,1,0:T(8,128)S(1)} %fusion.268, f32[4,256,16]{1,2,0:T(8,128)S(1)} %get-tuple-element.703, f32[4,256,256]{2,1,0:T(8,128)S(1)} %copy-done.63, f32[4,16,256]{2,1,0:T(8,128)S(1)} %copy-done.103, pred[4,256,256]{2,1,0:T(8,128)(4,1)S(1)} %copy-done.86, ...), kind=kOutput, calls=%fused_computation.143 | convolution fusion | flops 3241148416 | bytes 14090240 | tf_op jit(solution)/shard_map/jvp(chij,cjhp->cihp)/dot_general | solution.py:56
  505.3 8.1 copy.422
  529.0 20.5 %fusion.76 = f32[4,256,16,64]{1,3,2,0:T(8,128)} fusion(f32[4,16,64,256]{3,2,1,0:T(8,128)S(1)} %fusion.271, f32[4,256,16]{1,2,0:T(8,128)S(1)} %get-tuple-element.707, f32[4,256,256]{2,1,0:T(8,128)S(1)} %copy-done.61, f32[4,16,256]{2,1,0:T(8,128)S(1)} %copy-done.100, pred[4,256,256]{2,1,0:T(8,128)(4,1)S(1)} %copy-done.83, ...), kind=kOutput, calls=%fused_computation.136 | convolution fusion | flops 3241148416 | bytes 14090240 | tf_op jit(solution)/shard_map/jvp(chij,cjhp->cihp)/dot_general | solution.py:56
  565.2 13.4 multiply_reduce_fusion.21
  585.5 13.9 multiply_reduce_fusion.5
  606.2 11.9 multiply_reduce_fusion.7
  638.4 11.3 while.70
  657.8 11.0 multiply_reduce_fusion.6
  688.3 13.5 while.71
  705.7 18.8 %multiply_reduce_fusion.2 = (f32[4,256,16]{1,2,0:T(8,128)}, f32[4,256,16]{1,2,0:T(8,128)}, f32[4,256,16,64]{1,3,2,0:T(8,128)}) fusion(f32[4,256,16,64]{1,3,2,0:T(8,128)S(1)} %fusion.273, f32[4,256,16,64]{1,3,2,0:T(8,128)} %copy.325, f32[4,256,16]{1,2,0:T(8,128)S(1)} %bitcast.502, f32[4,256,256]{2,1,0:T(8,128)S(1)} %copy-done.62, ...), kind=kOutput, calls=%fused_computation.149 | convolution fusion | flops 3246358528 | bytes 18415616 | tf_op jit(solution)/shard_map/transpose(jvp(chij,cjhp->cihp))/dot_general | solution.py:56
  724.5 8.1 copy.439
  740.3 15.3 multiply_reduce_fusion.10
  755.6 17.3 %multiply_reduce_fusion.3 = (f32[4,256,16]{1,2,0:T(8,128)}, f32[4,256,16]{1,2,0:T(8,128)}, f32[4,256,16,64]{1,3,2,0:T(8,128)}) fusion(f32[4,256,16,64]{1,3,2,0:T(8,128)S(1)} %copy-done.48, f32[4,256,16,64]{1,3,2,0:T(8,128)S(1)} %copy-done.12, f32[4,256,16]{1,2,0:T(8,128)S(1)} %bitcast.507, f32[4,256,256]{2,1,0:T(8,128)S(1)} %copy-done.64, ...), kind=kOutput, calls=%fused_computation.150 | convolution fusion | flops 3246358528 | bytes 18415616 | tf_op jit(solution)/shard_map/transpose(jvp(chij,cjhp->cihp))/dot_general | solution.py:56
  773.0 8.1 copy.432
  788.8 13.9 multiply_reduce_fusion.14
  802.7 8.4 select_multiply_fusion
  811.1 11.4 fusion.45
  822.4 15.9 convolution_bitcast_fusion
  838.4 16.5 convolution_bitcast_fusion.1
  855.0 11.3 fusion.247
  867.0 11.5 fusion.246
  878.8 16.2 fusion.83
  895.0 17.7 %add_bitcast_fusion = f32[2,2048,1024]{1,2,0:T(8,128)} fusion(f32[2,1024,2048]{2,1,0:T(8,128)} %fusion.83, bf16[1024,2048]{1,0:T(8,128)(2,1)} %all-gather.18.cloned.1.call-done, f32[1,1024,1024]{2,1,0:T(8,128)} %get-tuple-element.731, f32[1,1024,1024]{2,1,0:T(8,128)S(1)} %copy-done.49), kind=kOutput, calls=%fused_computation.22 | convolution fusion | flops 8598323200 | bytes 46137344 | tf_op jit(solution)/shard_map/ld,kle->kde/dot_general | solution.py:171
  914.3 8.9 fusion.186
  923.3 27.3 %fusion.19 = (f32[4,16,256]{2,1,0:T(8,128)}, f32[4,16,256]{2,1,0:T(8,128)}, f32[4,256,256]{2,1,0:T(8,128)S(1)}) fusion(f32[4,256,256]{2,1,0:T(8,128)S(1)} %copy-done.65, f32[4,16,256]{2,1,0:T(8,128)S(1)} %copy-done.104, pred[4,256,256]{2,1,0:T(8,128)(4,1)S(1)} %copy-done.87, f32[4,256,16,64]{1,3,2,0:T(8,128)} %copy.311, f32[4,256,16]{1,2,0:T(8,128)S(1)} %bitcast.508, ...), kind=kOutput, calls=%fused_computation.38 | convolution fusion | flops 3268116480 | bytes 11010048 | tf_op jit(solution)/shard_map/transpose(jvp(chij,cjhp->cihp))/dot_general | solution.py:56
  953.0 9.1 fusion.180
  970.4 9.9 reduce-window.34
  980.6 9.0 fusion.189
  989.7 26.4 %fusion.21 = (f32[4,16,256]{2,1,0:T(8,128)}, f32[4,16,256]{2,1,0:T(8,128)}, f32[4,256,256]{2,1,0:T(8,128)S(1)}) fusion(f32[4,256,256]{2,1,0:T(8,128)} %fusion.270, f32[4,16,256]{2,1,0:T(8,128)S(1)} %copy-done.102, pred[4,256,256]{2,1,0:T(8,128)(4,1)S(1)} %copy-done.85, f32[4,256,16,64]{1,3,2,0:T(8,128)} %copy.325, f32[4,256,16]{1,2,0:T(8,128)S(1)} %bitcast.503, ...), kind=kOutput, calls=%fused_computation.40 | convolution fusion | flops 3268116480 | bytes 11010048 | tf_op jit(solution)/shard_map/transpose(jvp(chij,cjhp->cihp))/dot_general | solution.py:56
  1019.6 8.8 fusion.183
  1039.6 10.6 reduce-window.36
  1061.5 74.9 %all-reduce.70 = (bf16[1024,320]{0,1:T(8,128)(2,1)S(1)}, bf16[1024,320]{0,1:T(8,128)(2,1)}) all-reduce(f32[1024,320]{0,1:T(8,128)S(1)} %add_dynamic-update-slice_fusion, f32[1024,320]{0,1:T(8,128)S(1)} %add_dynamic-update-slice_fusion.1), channel_id=1, replica_groups=mesh['dp'=8,'tensor'=4] {'tensor'}, use_global_device_ids=true, to_apply=%region_44.46 | all-reduce | flops 655360 | bytes 3932160 | tf_op jit(solution)/shard_map/psum | solution.py:169
  1161.3 36.8 %all-reduce.65 = (f32[5,1024]{1,0:T(8,128)}, f32[16]{0:T(128)}, f32[16]{0:T(128)}, f32[16]{0:T(128)}, f32[1024]{0:T(1024)}) all-reduce(f32[5,1024]{1,0:T(8,128)S(1)} %add_add_fusion, f32[16]{0:T(128)} %add.478, f32[16]{0:T(128)S(1)} %add_multiply_fusion, f32[16]{0:T(128)S(1)} %add.480, ...), channel_id=1, replica_groups=mesh['dp'=8,'tensor'=4] {'dp'}, use_global_device_ids=true, to_apply=%region_61.63 | all-reduce | flops 6192 | bytes 49536 | tf_op jit(solution)/shard_map/psum | solution.py:199
  1207.0 40.1 %all-reduce.64 = (f32[2048]{0:T(1024)}, f32[5,256]{1,0:T(8,128)}) all-reduce(f32[2048]{0:T(1024)S(1)} %add.472, f32[5,256]{1,0:T(8,128)S(1)} %add_add_fusion.1), channel_id=1, replica_groups=mesh['dp'=8,'tensor'=4] {'dp','tensor'}, use_global_device_ids=true, to_apply=%region_48.50 | all-reduce | flops 3328 | bytes 26624 | tf_op jit(solution)/shard_map/psum | solution.py:200
  1255.9 184.8 %reduce-scatter.16.cloned.1.call-done = f32[2,256,1024]{1,2,0:T(8,128)} async-done(((f32[2,2048,1024]{1,2,0:T(8,128)}), f32[2,256,1024]{1,2,0:T(8,128)}) %reduce-scatter.16.cloned.1.call-update) | async-done | bytes 2097168 | tf_op jit(solution)/shard_map/reduce_scatter | solution.py:195
  1443.6 71.6 %reduce-scatter.18.cloned.1.call-done = f32[256,320]{0,1:T(8,128)} async-done(((f32[2048,320]{0,1:T(8,128)}), f32[256,320]{0,1:T(8,128)}) %reduce-scatter.18.cloned.1.call-update) | async-done | bytes 327696 | tf_op jit(solution)/shard_map/reduce_scatter | solution.py:196
  1515.1 152.8 %reduce-scatter.20.cloned.1.call-done = f32[1024,256]{1,0:T(8,128)} async-done(((f32[1024,2048]{1,0:T(8,128)}), f32[1024,256]{1,0:T(8,128)}) %reduce-scatter.20.cloned.1.call-update) | async-done | bytes 1048592 | tf_op jit(solution)/shard_map/reduce_scatter | solution.py:197
  (690 shorter events, 367.7 us)
Async XLA Ops:
  7.2 47.8 %all-gather.14.cloned.1.call-start = ((), (), s32[]{:S(2)}) async-start(), calls=%async_computation.9 | async-start | bytes 1474560 | tf_op jit(solution)/shard_map/all_gather | solution.py:127
  7.9 82.3 %all-gather.18.cloned.1.call-start = ((), (), s32[]{:S(2)}) async-start(), calls=%async_computation.12 | async-start | bytes 5242880 | tf_op jit(solution)/shard_map/all_gather | solution.py:135
  14.7 112.2 %all-gather.10.cloned.1.call-start = ((), (), s32[]{:S(2)}) async-start(), calls=%async_computation.7 | async-start | bytes 5242880 | tf_op jit(solution)/shard_map/all_gather | solution.py:135
  15.5 148.4 %all-gather.22.cloned.1.call-start = ((), (), s32[]{:S(2)}) async-start(), calls=%async_computation.20 | async-start | bytes 5242880 | tf_op jit(solution)/shard_map/all_gather | solution.py:136
  17.0 223.3 %all-gather.16.cloned.1.call-start = ((), (), s32[]{:S(2)}) async-start(), calls=%async_computation.10 | async-start | bytes 4718592 | tf_op jit(solution)/shard_map/all_gather | solution.py:128
  17.6 347.9 %all-gather.12.cloned.1.call-start = ((), (), s32[]{:S(2)}) async-start(), calls=%async_computation.8 | async-start | bytes 9437184 | tf_op jit(solution)/shard_map/all_gather | solution.py:126
  18.2 567.3 %all-gather.20.cloned.1.call-start = ((), (), s32[]{:S(2)}) async-start(), calls=%async_computation.19 | async-start | bytes 5242880 | tf_op jit(solution)/shard_map/all_gather | solution.py:136
  19.0 1179.3 %reduce-scatter.14.cloned.1.call-start = ((), (), s32[]{:S(2)}) async-start(), calls=%async_computation.15 | async-start | bytes 10485760 | tf_op jit(solution)/shard_map/reduce_scatter | solution.py:178
  21.2 109.6 %copy-start.195 = (f32[16]{0:T(128)}, f32[16]{0:T(128)S(1)}, u32[]{:S(2)}) copy-start(f32[16]{0:T(128)S(1)} %exponential_negate_fusion) | copy-start | bytes 196
  54.9 72.0 %copy-start.59 = (bf16[2048,320]{0,1:T(8,128)(2,1)S(1)}, bf16[2048,320]{0,1:T(8,128)(2,1)}, u32[]{:S(2)}) copy-start(bf16[2048,320]{0,1:T(8,128)(2,1)} %all-gather.14.cloned.1.call-done) | copy-start | bytes 3932164
  95.6 45.3 %copy-start.25 = (f32[1024,256]{0,1:T(8,128)}, f32[1024,256]{0,1:T(8,128)S(1)}, u32[]{:S(2)}) copy-start(f32[1024,256]{0,1:T(8,128)S(1)} %slice.309) | copy-start | bytes 3145732
  95.6 36.2 %copy-start.193 = (f32[16]{0:T(128)S(1)}, f32[16]{0:T(128)}, u32[]{:S(2)}) copy-start(f32[16]{0:T(128)} %param.28) | copy-start | bytes 196
  137.9 567.8 %copy-start.74 = (f32[2,4,8,256]{3,2,0,1:T(8,128)}, f32[2,4,8,256]{3,2,0,1:T(8,128)S(1)}, u32[]{:S(2)}) copy-start(f32[2,4,8,256]{3,2,0,1:T(8,128)S(1)} %copy.542) | copy-start | bytes 196612
  155.4 95.0 %copy-start.32 = (f32[4,256,128]{2,1,0:T(8,128)}, f32[4,256,128]{2,1,0:T(8,128)S(1)}, u32[]{:S(2)}) copy-start(f32[4,256,128]{2,1,0:T(8,128)S(1)} %copy.332) | copy-start | bytes 1572868
  158.4 470.7 %copy-start.72 = (f32[4,256,16]{1,2,0:T(8,128)}, f32[4,256,16]{1,2,0:T(8,128)S(1)}, u32[]{:S(2)}) copy-start(f32[4,256,16]{1,2,0:T(8,128)S(1)} %get-tuple-element.703) | copy-start | bytes 196612
  158.4 597.2 %copy-start.70 = (f32[4,256,16]{1,2,0:T(8,128)}, f32[4,256,16]{1,2,0:T(8,128)S(1)}, u32[]{:S(2)}) copy-start(f32[4,256,16]{1,2,0:T(8,128)S(1)} %get-tuple-element.704) | copy-start | bytes 196612
  159.9 519.9 %copy-start.68 = (f32[4,256,16]{1,2,0:T(8,128)}, f32[4,256,16]{1,2,0:T(8,128)S(1)}, u32[]{:S(2)}) copy-start(f32[4,256,16]{1,2,0:T(8,128)S(1)} %get-tuple-element.707) | copy-start | bytes 196612
  159.9 545.8 %copy-start.66 = (f32[4,256,16]{1,2,0:T(8,128)}, f32[4,256,16]{1,2,0:T(8,128)S(1)}, u32[]{:S(2)}) copy-start(f32[4,256,16]{1,2,0:T(8,128)S(1)} %get-tuple-element.708) | copy-start | bytes 196612
  838.3 363.7 %reduce-scatter.12.cloned.1.call-start = ((), (), s32[]{:S(2)}) async-start(), calls=%async_computation.14 | async-start | bytes 10485760 | tf_op jit(solution)/shard_map/reduce_scatter | solution.py:178
  855.0 392.2 %reduce-scatter.10.cloned.1.call-start = ((), (), s32[]{:S(2)}) async-start(), calls=%async_computation.13 | async-start | bytes 10485760 | tf_op jit(solution)/shard_map/reduce_scatter | solution.py:148
  866.3 380.8 %reduce-scatter.8.cloned.1.call-start = ((), (), s32[]{:S(2)}) async-start(), calls=%async_computation.11 | async-start | bytes 10485760 | tf_op jit(solution)/shard_map/reduce_scatter | solution.py:148
  878.5 562.1 %reduce-scatter.16.cloned.1.call-start = ((), (), s32[]{:S(2)}) async-start(), calls=%async_computation.16 | async-start | bytes 18874368 | tf_op jit(solution)/shard_map/reduce_scatter | solution.py:195
  912.8 602.4 %reduce-scatter.18.cloned.1.call-start = ((), (), s32[]{:S(2)}) async-start(), calls=%async_computation.17 | async-start | bytes 2949120 | tf_op jit(solution)/shard_map/reduce_scatter | solution.py:196
  923.2 27.4 %copy-start.37 = (f32[4,256,128]{2,1,0:T(8,128)S(1)}, f32[4,256,128]{2,1,0:T(8,128)}, u32[]{:S(2)}) copy-start(f32[4,256,128]{2,1,0:T(8,128)} %copy-done.36) | copy-start | bytes 1572868
  923.2 29.5 %copy-start.99 = (f32[4,16]{1,0:T(4,128)S(1)}, f32[4,16]{1,0:T(4,128)}, u32[]{:S(2)}) copy-start(f32[4,16]{1,0:T(4,128)} %slice_reduce_fusion.1) | copy-start | bytes 772
  923.2 29.5 %copy-start.173 = (f32[4,16]{1,0:T(4,128)S(1)}, f32[4,16]{1,0:T(4,128)}, u32[]{:S(2)}) copy-start(f32[4,16]{1,0:T(4,128)} %copy-done.172) | copy-start | bytes 772
  923.2 29.5 %copy-start.177 = (pred[4]{0:T(512)(128)(4,1)S(1)}, pred[4]{0:T(512)(128)(4,1)}, u32[]{:S(2)}) copy-start(pred[4]{0:T(512)(128)(4,1)} %compare_reduce_fusion.1) | copy-start | bytes 16
  923.2 29.6 %copy-start.71 = (f32[4,256,16]{1,2,0:T(8,128)S(1)}, f32[4,256,16]{1,2,0:T(8,128)}, u32[]{:S(2)}) copy-start(f32[4,256,16]{1,2,0:T(8,128)} %copy-done.70) | copy-start | bytes 196612
  989.6 26.4 %copy-start.33 = (f32[4,256,128]{2,1,0:T(8,128)S(1)}, f32[4,256,128]{2,1,0:T(8,128)}, u32[]{:S(2)}) copy-start(f32[4,256,128]{2,1,0:T(8,128)} %copy-done.32) | copy-start | bytes 1572868
  989.7 28.5 %copy-start.97 = (f32[4,16]{1,0:T(4,128)S(1)}, f32[4,16]{1,0:T(4,128)}, u32[]{:S(2)}) copy-start(f32[4,16]{1,0:T(4,128)} %copy-done.96) | copy-start | bytes 772
  989.7 28.5 %copy-start.175 = (pred[4]{0:T(512)(128)(4,1)S(1)}, pred[4]{0:T(512)(128)(4,1)}, u32[]{:S(2)}) copy-start(pred[4]{0:T(512)(128)(4,1)} %compare_reduce_fusion) | copy-start | bytes 16
  989.7 29.9 %copy-start.67 = (f32[4,256,16]{1,2,0:T(8,128)S(1)}, f32[4,256,16]{1,2,0:T(8,128)}, u32[]{:S(2)}) copy-start(f32[4,256,16]{1,2,0:T(8,128)} %copy-done.66) | copy-start | bytes 196612
  1143.8 524.2 %reduce-scatter.20.cloned.1.call-start = ((), (), s32[]{:S(2)}) async-start(), calls=%async_computation.18 | async-start | bytes 9437184 | tf_op jit(solution)/shard_map/reduce_scatter | solution.py:197
  1159.1 39.1 %copy-start.178 = (f32[256]{0:T(256)S(1)}, f32[256]{0:T(256)}, u32[]{:S(2)}) copy-start(f32[256]{0:T(256)} %get-tuple-element.560) | copy-start | bytes 3076
  1159.1 39.0 %copy-start.179 = (f32[256]{0:T(256)S(1)}, f32[256]{0:T(256)}, u32[]{:S(2)}) copy-start(f32[256]{0:T(256)} %get-tuple-element.566) | copy-start | bytes 3076
  1159.1 39.0 %copy-start.180 = (f32[256]{0:T(256)S(1)}, f32[256]{0:T(256)}, u32[]{:S(2)}) copy-start(f32[256]{0:T(256)} %get-tuple-element.567) | copy-start | bytes 3076
  1159.1 39.0 %copy-start.181 = (f32[256]{0:T(256)S(1)}, f32[256]{0:T(256)}, u32[]{:S(2)}) copy-start(f32[256]{0:T(256)} %get-tuple-element.561) | copy-start | bytes 3076
  1159.1 39.0 %copy-start.182 = (f32[256]{0:T(256)S(1)}, f32[256]{0:T(256)}, u32[]{:S(2)}) copy-start(f32[256]{0:T(256)} %get-tuple-element.562) | copy-start | bytes 3076
  1159.1 39.0 %copy-start.183 = (f32[256]{0:T(256)S(1)}, f32[256]{0:T(256)}, u32[]{:S(2)}) copy-start(f32[256]{0:T(256)} %get-tuple-element.563) | copy-start | bytes 3076
  1159.1 39.0 %copy-start.184 = (f32[256]{0:T(256)S(1)}, f32[256]{0:T(256)}, u32[]{:S(2)}) copy-start(f32[256]{0:T(256)} %get-tuple-element.568) | copy-start | bytes 3076
  1159.2 39.0 %copy-start.185 = (f32[256]{0:T(256)S(1)}, f32[256]{0:T(256)}, u32[]{:S(2)}) copy-start(f32[256]{0:T(256)} %get-tuple-element.569) | copy-start | bytes 3076
  1159.2 39.1 %copy-start.60 = (bf16[2048,320]{0,1:T(8,128)(2,1)S(1)}, bf16[2048,320]{0,1:T(8,128)(2,1)}, u32[]{:S(2)}) copy-start(bf16[2048,320]{0,1:T(8,128)(2,1)} %all-gather.14.cloned.1.call-done) | copy-start | bytes 3932164
  1159.2 42.8 %copy-start.18 = (bf16[2,256,2048]{2,1,0:T(8,128)(2,1)S(1)}, bf16[2,256,2048]{2,1,0:T(8,128)(2,1)}, u32[]{:S(2)}) copy-start(bf16[2,256,2048]{2,1,0:T(8,128)(2,1)} %param.22) | copy-start | bytes 6291460
  1159.2 42.8 %copy-start.136 = (f32[2048]{0:T(1024)S(1)}, f32[2048]{0:T(1024)}, u32[]{:S(2)}) copy-start(f32[2048]{0:T(1024)} %param.23) | copy-start | bytes 24580
  1159.2 42.8 %copy-start.168 = (f32[256]{0:T(256)S(1)}, f32[256]{0:T(256)}, u32[]{:S(2)}) copy-start(f32[256]{0:T(256)} %copy-done.167) | copy-start | bytes 3076
  1159.2 42.8 %copy-start.170 = (f32[256]{0:T(256)S(1)}, f32[256]{0:T(256)}, u32[]{:S(2)}) copy-start(f32[256]{0:T(256)} %copy-done.169) | copy-start | bytes 3076
  1202.0 45.2 %copy-start.186 = (f32[256]{0:T(256)S(1)}, f32[256]{0:T(256)}, u32[]{:S(2)}) copy-start(f32[256]{0:T(256)} %get-tuple-element.758) | copy-start | bytes 3076
  1202.0 45.2 %copy-start.187 = (f32[256]{0:T(256)S(1)}, f32[256]{0:T(256)}, u32[]{:S(2)}) copy-start(f32[256]{0:T(256)} %get-tuple-element.767) | copy-start | bytes 3076
  (172 other events, 1389.4 us)
Sparse Core Ops, SparseCore 0:
  10.1 44.8 all-gather.13
  57.1 33.1 all-gather.17
  92.4 34.4 all-gather.9
  128.9 34.4 all-gather.21
  165.3 75.0 all-gather.15
  242.4 123.0 all-gather.11
  367.1 32.6 all-gather.19
  838.5 69.4 reduce-scatter.13
  910.7 71.6 reduce-scatter.11
  984.9 71.6 reduce-scatter.9
  1059.4 94.8 reduce-scatter.7
  1158.0 282.6 reduce-scatter.15
  1445.2 69.9 reduce-scatter.17
  1519.6 148.2 reduce-scatter.19
where the time goes:
time: 1680 us; the launch traced here: 1670 us
  waiting for transfers between devices  699 us (42%)
  matrix products  401 us (24%)
  other arithmetic  203 us (12%)
  local copies, waits for them, and re-layouts  189 us (11%)
  blocking collectives  164 us (10%)
  between operations  17.2 us (1%)
    reduce_scatter x1, waiting for transfers between devices, local(): lax.psum_scatter(grad_zx, 'dp', scatter_dimension=1, tiled=True)  185 us
    reduce_scatter x1, waiting for transfers between devices, local(): lax.psum_scatter(grad_out, 'dp', scatter_dimension=1, tiled=True)  153 us
    dot_general x6, matrix products, state_space(): jnp.einsum('chij,cjhp->cihp', decay * scores[:, None], weighted, precisio...  131 us
    all_gather x1, waiting for transfers between devices, local(): lax.all_gather(w_zx, 'dp', axis=1, tiled=True)  115 us
    all_gather x1, waiting for transfers between devices, local(): lax.all_gather(w_out, 'dp', axis=1, tiled=True)  76.5 us
    psum x1, blocking collectives, local(): d_bcdt_low = lax.psum(d_bcdt_part, 'tensor').astype(jnp.bfloat16)  74.9 us
    reduce_scatter x1, waiting for transfers between devices, local(): lax.psum_scatter(grad_bcdt, 'dp', scatter_dimension=0, tiled=True)  71.6 us
    all_gather x2, waiting for transfers between devices, local(): lax.all_gather(u_piece, 'tensor', axis=0, tiled=True)  66.6 us
  transfers between devices with their start and end apart: 14, of which 8 were waited for; matrix products, arithmetic and copies ran while one was open for 32% of the time, Pallas kernels for 0%

commit v1 on v0

v1 whole, which is shorter than its diff:
```python
import functools

import jax
import jax.numpy as jnp
import numpy as np
from jax import lax
from jax.experimental import pallas as pl
from jax.experimental.pallas import tpu as pltpu
from jax.sharding import PartitionSpec as P

MESH = pl.DeviceIdType.MESH
EPS = 1e-05
BLOCK = 256
F32 = jnp.float32
BF16 = jnp.bfloat16
EXACT = lax.Precision.HIGHEST
LOG2E = 1.4426950408889634
NEG = -1e30


def sigmoid(v):
    return 0.5 * jnp.tanh(0.5 * v) + 0.5


def split3(v):
    hi = v.astype(BF16)
    rest = v - hi.astype(F32)
    mid = rest.astype(BF16)
    low = (rest - mid.astype(F32)).astype(BF16)
    return hi, mid, low


def dot(a, b):
    return jnp.dot(a, b, preferred_element_type=F32)


def dot_nt(a, b):
    return lax.dot_general(a, b, (((1,), (1,)), ((), ())), preferred_element_type=F32)


def dot_tn(a, b):
    return lax.dot_general(a, b, (((0,), (0,)), ((), ())), preferred_element_type=F32)


def softplus(v):
    return jnp.maximum(v, 0.0) + jnp.log1p(jnp.exp(-jnp.abs(v)))


def head_sizes(raw, dt_bias, a_log):
    q = raw.shape[0]
    tri = (
        lax.broadcasted_iota(jnp.int32, (q, q), 0) >= lax.broadcasted_iota(jnp.int32, (q, q), 1)
    ).astype(F32)
    biased = raw + dt_bias
    step = softplus(biased)
    rate = -jnp.exp(a_log) * step
    cum = jnp.dot(tri, rate, precision=EXACT, preferred_element_type=F32) * LOG2E
    return biased, step, rate, cum


def expand(values, spread):
    hi, mid, low = split3(values)
    return dot(hi, spread) + dot(mid, spread) + dot(low, spread)


def gather_heads(values, spread):
    hi, mid, _ = split3(values)
    return dot_nt(hi, spread) + dot_nt(mid, spread)


def exact_nt(a, b):
    a_hi, a_mid, _ = split3(a)
    b_hi, b_mid, _ = split3(b)
    return dot_nt(a_hi, b_hi) + dot_nt(a_hi, b_mid) + dot_nt(a_mid, b_hi)


def transpose_heads(values):
    pad = jnp.concatenate(
        [values, jnp.zeros((values.shape[0], 128 - values.shape[1]), F32)], axis=1
    )
    return pad.T


def forward_kernel(
    x_ref, bc_ref, dt_ref, cols_ref, segrow_ref, taps_x_ref, taps_bc_ref, bias_ref, alog_ref, skip_ref, spread_ref,
    y_ref, cx_ref, cbc_ref, states_ref,
    xs, bs, state, mask_bias,
):
    block = pl.program_id(1)
    q = BLOCK
    heads = dt_ref.shape[-1]
    channels = x_ref.shape[-1]
    width = channels // heads

    @pl.when(block == 0)
    def _():
        xs[0:8, :] = jnp.zeros((8, xs.shape[1]), F32)
        bs[0:8, :] = jnp.zeros((8, bs.shape[1]), F32)
        state[...] = jnp.zeros_like(state)

    cols = cols_ref[0]
    lag_masks = [cols[:, k : k + 1] for k in range(3)]
    reads, last, seg = cols[:, 3:4], cols[:, 4:5], cols[:, 5:6]

    def conv(value_ref, hold, taps_ref):
        hold[8 : 8 + q, :] = value_ref[0]
        out = taps_ref[4:5, :] + taps_ref[3:4, :] * hold[8 : 8 + q, :]
        for lag in (1, 2, 3):
            out = out + (lag_masks[lag - 1] * hold[8 - lag : 8 - lag + q, :]) * taps_ref[3 - lag : 4 - lag, :]
        hold[0:8, :] = hold[q : q + 8, :]
        return out

    cbc = conv(bc_ref, bs, taps_bc_ref)
    cbc_ref[0] = cbc
    bc = cbc * sigmoid(cbc)
    n = bc.shape[1] // 2
    scores = exact_nt(bc[:, n:], bc[:, :n])
    b_mat, c_mat = bc[:, :n].astype(BF16), bc[:, n:].astype(BF16)

    cx = conv(x_ref, xs, taps_x_ref)
    cx_ref[0] = cx
    xb = (cx * sigmoid(cx)).astype(BF16)

    biased, step, rate, cum = head_sizes(dt_ref[0], bias_ref[...], alog_ref[...])
    cum_end = cum[q - 1 : q, :]
    spread = spread_ref[...]
    reads_e = expand(reads * jnp.exp2(cum), spread)
    to_end_e = expand(last * jnp.exp2(cum_end - cum) * step, spread)
    carry = jnp.exp2(cum_end)
    carry_e = expand(jnp.broadcast_to(carry, (8, heads)), spread)[0:1]
    source = transpose_heads(cum - jnp.log(step) * LOG2E)

    rows = lax.broadcasted_iota(jnp.int32, (q, q), 0)
    places = lax.broadcasted_iota(jnp.int32, (q, q), 1)
    mask_bias[...] = jnp.where((seg == segrow_ref[0]) & (rows >= places), 0.0, NEG)

    st = state[...].astype(BF16)
    states_ref[0, 0] = st
    outside = dot(c_mat, st) * reads_e + skip_ref[...] * xb.astype(F32)

    half = q // 2
    lane = lax.broadcasted_iota(jnp.int32, (1, 2 * width), 1)
    for pair in range(heads // 2):
        at = slice(pair * 2 * width, (pair + 1) * 2 * width)
        xp = xb[:, at]
        both = []
        for h in (2 * pair, 2 * pair + 1):
            col = cum[:, h : h + 1]
            row = source[h : h + 1, :]
            top = (
                jnp.exp2((col[:half] - row[:, :half]) + mask_bias[:half, :half]) * scores[:half, :half]
            ).astype(BF16)
            low = (jnp.exp2((col[half:] - row) + mask_bias[half:, :]) * scores[half:, :]).astype(BF16)
            both.append(jnp.concatenate([dot(top, xp[:half]), dot(low, xp)], axis=0))
        y_ref[0, :, at] = outside[:, at] + jnp.where(lane < width, both[0], both[1])

    scaled = (xb.astype(F32) * to_end_e).astype(BF16)
    state[...] = carry_e * state[...] + dot_tn(b_mat, scaled)


def backward_kernel(
    dy_ref, x_ref, cx_ref, bc_ref, cbc_ref, dt_ref, cols_ref, segrow_ref, states_ref,
    taps_x_ref, taps_bc_ref, bias_ref, alog_ref, skip_ref, spread_ref,
    dx_ref, dbc_ref, ddt_ref, gx_ref, gbc_ref, gh_ref,
    ds_x, ds_bc, d_state, mask_bias, d_scores, d_in, row_sums,
):
    seq, step_id = pl.program_id(0), pl.program_id(1)
    q = BLOCK
    heads = dt_ref.shape[-1]
    channels = x_ref.shape[-1]
    width = channels // heads

    @pl.when(step_id == 0)
    def _():
        ds_x[:, q : q + 8, :] = jnp.zeros((4, 8, channels), F32)
        ds_bc[:, q : q + 8, :] = jnp.zeros((4, 8, ds_bc.shape[2]), F32)
        d_state[...] = jnp.zeros_like(d_state)

    @pl.when((step_id == 0) & (seq == 0))
    def _():
        gx_ref[...] = jnp.zeros_like(gx_ref)
        gbc_ref[...] = jnp.zeros_like(gbc_ref)
        gh_ref[...] = jnp.zeros_like(gh_ref)

    cols = cols_ref[0]
    lag_masks = [cols[:, k : k + 1] for k in range(3)]
    reads, last, seg = cols[:, 3:4], cols[:, 4:5], cols[:, 5:6]

    cbc = cbc_ref[0]
    sig_bc = sigmoid(cbc)
    bc = cbc * sig_bc
    n = bc.shape[1] // 2
    scores = exact_nt(bc[:, :n], bc[:, n:])
    b_mat, c_mat = bc[:, :n].astype(BF16), bc[:, n:].astype(BF16)
    cx = cx_ref[0]
    sig_x = sigmoid(cx)
    xc = cx * sig_x
    xb = xc.astype(BF16)
    xbf = xb.astype(F32)
    dyb = dy_ref[0]
    dyf = dyb.astype(F32)

    biased, step, rate, cum = head_sizes(dt_ref[0], bias_ref[...], alog_ref[...])
    cum_end = cum[q - 1 : q, :]
    spread = spread_ref[...]
    reads_e = expand(reads * jnp.exp2(cum), spread)
    to_end_e = expand(last * jnp.exp2(cum_end - cum) * step, spread)
    carry_e = expand(jnp.broadcast_to(jnp.exp2(cum_end), (8, heads)), spread)[0:1]
    source = cum - jnp.log(step) * LOG2E
    target = transpose_heads(cum)

    rows = lax.broadcasted_iota(jnp.int32, (q, q), 0)
    places = lax.broadcasted_iota(jnp.int32, (q, q), 1)
    mask_bias[...] = jnp.where((seg == segrow_ref[0]) & (rows <= places), 0.0, NEG)

    st = states_ref[0, 0]
    dst = d_state[...].astype(BF16)
    dye = (dyf * reads_e).astype(BF16)
    scaled = (xbf * to_end_e).astype(BF16)
    d_c = dot_nt(dye, st)
    d_b = dot_nt(scaled, dst)
    dx_st = dot(b_mat, dst) * to_end_e
    carried = carry_e * jnp.sum(d_state[...] * st.astype(F32), axis=0, keepdims=True)
    out_part = dyf * reads_e * dot(c_mat, st)
    d_state[...] = carry_e * d_state[...] + dot_tn(c_mat, dye)

    half = q // 2
    lane = lax.broadcasted_iota(jnp.int32, (1, 2 * width), 1)
    d_scores[...] = jnp.zeros_like(d_scores)
    head_lane = lax.broadcasted_iota(jnp.int32, (1, heads), 1)
    col_sums = jnp.zeros((q, heads), F32)
    for pair in range(heads // 2):
        at = slice(pair * 2 * width, (pair + 1) * 2 * width)
        xp, dyp = xb[:, at], dyb[:, at]
        both = []
        for which in (0, 1):
            h = 2 * pair + which
            mine = lane < width if which == 0 else lane >= width
            xm = jnp.where(mine, xp, jnp.zeros_like(xp))
            col = source[:, h : h + 1]
            row = target[h : h + 1, :]
            top = jnp.exp2((row - col[:half]) + mask_bias[:half, :])
            low = jnp.exp2((row[:, half:] - col[half:]) + mask_bias[half:, half:])
            d_top = top * dot_nt(xm[:half], dyp)
            d_low = low * dot_nt(xm[half:], dyp[half:])
            d_scores[:half, :] += d_top
            d_scores[half:, half:] += d_low
            m_top = d_top * scores[:half, :]
            m_low = d_low * scores[half:, half:]
            late = jnp.sum(m_top[:, half:], axis=0, keepdims=True) + jnp.sum(m_low, axis=0, keepdims=True)
            row_sums[h : h + 1, :half] = jnp.sum(m_top[:, :half], axis=0, keepdims=True)
            row_sums[h : h + 1, half:] = late
            here = jnp.concatenate(
                [
                    jnp.sum(m_top[:, :half] + m_top[:, half:], axis=1, keepdims=True),
                    jnp.sum(m_low, axis=1, keepdims=True),
                ],
                axis=0,
            )
            col_sums = jnp.where(head_lane == h, here, col_sums)
            top = (top * scores[:half, :]).astype(BF16)
            low = (low * scores[half:, half:]).astype(BF16)
            both.append(jnp.concatenate([dot(top, dyp), dot(low, dyp[half:])], axis=0))
        d_in[:, at] = jnp.where(lane < width, both[0], both[1])

    dsb = d_scores[...].astype(BF16)
    d_b = d_b + dot(dsb, c_mat)
    d_c = d_c + dot_tn(dsb, b_mat)

    dx = d_in[...] + dx_st
    skip = skip_ref[...]
    state_h = gather_heads(xbf * dx_st, spread)
    used_h = col_sums + state_h
    diff_h = row_sums[...].T[:, :heads] - col_sums + gather_heads(out_part, spread)
    from_here = (rows <= places).astype(F32)
    before = (rows > places).astype(F32)
    d_rate = (
        jnp.dot(from_here, diff_h, precision=EXACT, preferred_element_type=F32)
        + jnp.dot(before, state_h, precision=EXACT, preferred_element_type=F32)
        + gather_heads(jnp.broadcast_to(carried, (8, channels)), spread)[0:1]
    )
    sig_dt = sigmoid(biased)
    ratio = jnp.where(step < 1e-30, 1.0, sig_dt / jnp.maximum(step, 1e-30))
    d_raw = used_h * ratio - jnp.exp(alog_ref[...]) * sig_dt * d_rate
    ddt_ref[0] = d_raw
    gh_ref[0:1, :heads] += jnp.sum(d_raw, axis=0, keepdims=True)
    gh_ref[1:2, :heads] += jnp.sum(d_rate * rate, axis=0, keepdims=True)

    def conv_back(d_out, value_ref, hold, taps_ref, grad_ref):
        value = value_ref[0]
        d_value = d_out * taps_ref[3:4, :]
        grad_ref[3:4, :] += jnp.sum(value * d_out, axis=0, keepdims=True)
        grad_ref[4:5, :] += jnp.sum(d_out, axis=0, keepdims=True)
        for lag in (1, 2, 3):
            hold[lag, 0:q, :] = lag_masks[lag - 1] * d_out
            moved = hold[lag, lag : lag + q, :]
            d_value = d_value + moved * taps_ref[3 - lag : 4 - lag, :]
            grad_ref[3 - lag : 4 - lag, :] += jnp.sum(value * moved, axis=0, keepdims=True)
            hold[lag, q : q + 8, :] = hold[lag, 0:8, :]
        return d_value

    d_bc = jnp.concatenate([d_b, d_c], axis=1) * (sig_bc * (1.0 + cbc * (1.0 - sig_bc)))
    dbc_ref[0] = conv_back(d_bc, bc_ref, ds_bc, taps_bc_ref, gbc_ref)
    gx_ref[5:6, :] += jnp.sum(dyf * xbf, axis=0, keepdims=True)
    d_cx = (dx + skip * dyf) * (sig_x * (1.0 + cx * (1.0 - sig_x)))
    dx_ref[0] = conv_back(d_cx, x_ref, ds_x, taps_x_ref, gx_ref).astype(BF16)


def column_masks(segments):
    seqs, length = segments.shape
    blocks = length // BLOCK
    lags = []
    for lag in (1, 2, 3):
        earlier = jnp.pad(segments, ((0, 0), (lag, 0)), constant_values=-1)[:, :length]
        lags.append(earlier == segments)
    grouped = segments.reshape(seqs, blocks, BLOCK)
    before = jnp.pad(segments, ((0, 0), (1, 0)), constant_values=-1)[:, :length].reshape(seqs, blocks, BLOCK)
    reads = (grouped == before[:, :, :1]).reshape(seqs, length)
    last = (grouped == grouped[:, :, -1:]).reshape(seqs, length)
    stacked = [m.astype(F32) for m in (*lags, reads, last, segments)]
    stacked += [jnp.zeros_like(stacked[0])] * 2
    return jnp.stack(stacked, axis=-1)


def spread_matrix(heads, channels):
    width = channels // heads
    return (np.arange(heads)[:, None] == np.arange(channels)[None, :] // width).astype(np.float32)


def shared_specs(channels, n2, heads):
    full = lambda *shape: pl.BlockSpec(shape, lambda s, c: (0,) * len(shape))
    return [full(5, channels), full(5, n2), full(1, heads), full(1, heads), full(1, channels), full(heads, channels)]


def ssd_forward(x, bc, dt, cols, segrow, shared):
    seqs, length, channels = x.shape
    n2, heads = bc.shape[2], dt.shape[2]
    blocks = length // BLOCK
    tok = lambda w: pl.BlockSpec((1, BLOCK, w), lambda s, c: (s, c, 0))
    return pl.pallas_call(
        forward_kernel,
        grid=(seqs, blocks),
        in_specs=[tok(channels), tok(n2), tok(heads), tok(8), pl.BlockSpec((1, 1, BLOCK), lambda s, c: (s, 0, c))]
        + shared_specs(channels, n2, heads),
        out_specs=[tok(channels), tok(channels), tok(n2),
                   pl.BlockSpec((1, 1, n2 // 2, channels), lambda s, c: (s, c, 0, 0))],
        out_shape=[
            jax.ShapeDtypeStruct((seqs, length, channels), F32),
            jax.ShapeDtypeStruct((seqs, length, channels), F32),
            jax.ShapeDtypeStruct((seqs, length, n2), F32),
            jax.ShapeDtypeStruct((seqs, blocks, n2 // 2, channels), BF16),
        ],
        scratch_shapes=[
            pltpu.VMEM((BLOCK + 8, channels), F32),
            pltpu.VMEM((BLOCK + 8, n2), F32),
            pltpu.VMEM((n2 // 2, channels), F32),
            pltpu.VMEM((BLOCK, BLOCK), F32),
        ],
        compiler_params=pltpu.CompilerParams(vmem_limit_bytes=48 * 2**20),
        name="ssd_forward",
    )(x, bc, dt, cols, segrow, *shared)


def ssd_backward(dy, x, cx, bc, cbc, dt, cols, segrow, states, shared):
    seqs, length, channels = x.shape
    n2, heads = bc.shape[2], dt.shape[2]
    blocks = length // BLOCK
    tok = lambda w: pl.BlockSpec((1, BLOCK, w), lambda s, c: (s, blocks - 1 - c, 0))
    whole = lambda *shape: pl.BlockSpec(shape, lambda s, c: (0,) * len(shape))
    return pl.pallas_call(
        backward_kernel,
        grid=(seqs, blocks),
        in_specs=[tok(channels)] * 3 + [tok(n2)] * 2 + [tok(heads), tok(8),
                  pl.BlockSpec((1, 1, BLOCK), lambda s, c: (s, 0, blocks - 1 - c)),
                  pl.BlockSpec((1, 1, n2 // 2, channels), lambda s, c: (s, blocks - 1 - c, 0, 0))]
        + shared_specs(channels, n2, heads),
        out_specs=[tok(channels), tok(n2), tok(heads), whole(8, channels), whole(8, n2), whole(8, 128)],
        out_shape=[
            jax.ShapeDtypeStruct((seqs, length, channels), BF16),
            jax.ShapeDtypeStruct((seqs, length, n2), F32),
            jax.ShapeDtypeStruct((seqs, length, heads), F32),
            jax.ShapeDtypeStruct((8, channels), F32),
            jax.ShapeDtypeStruct((8, n2), F32),
            jax.ShapeDtypeStruct((8, 128), F32),
        ],
        scratch_shapes=[
            pltpu.VMEM((4, BLOCK + 8, channels), F32),
            pltpu.VMEM((4, BLOCK + 8, n2), F32),
            pltpu.VMEM((n2 // 2, channels), F32),
            pltpu.VMEM((BLOCK, BLOCK), F32),
            pltpu.VMEM((BLOCK, BLOCK), F32),
            pltpu.VMEM((BLOCK, channels), F32),
            pltpu.VMEM((128, BLOCK), F32),
        ],
        compiler_params=pltpu.CompilerParams(vmem_limit_bytes=56 * 2**20),
        name="ssd_backward",
    )(dy, x, cx, bc, cbc, dt, cols, segrow, states, *shared)


def ring_place(n):
    dp = lax.axis_index("dp")
    z, y = dp // 2, dp % 2

    def at(place):
        q = (place + 4 * n) % n
        return 2 * q + (q // (n // 2)) * (2 * n - 1 - 4 * q)

    return z + y * (n - 1 - 2 * z), at


def tensor_place():
    t = lax.axis_index("tensor")
    return t, t + 1 - 2 * (t % 2), (t + 2) % 4


def greet(n):
    place, at = ring_place(n)
    _, other, across = tensor_place()
    sem = pltpu.get_barrier_semaphore()
    for target in ({"dp": at(place + 1)}, {"dp": at(place - 1)}, {"tensor": other}, {"tensor": across}):
        pl.semaphore_signal(sem, inc=1, device_id=target, device_id_type=MESH)
    pl.semaphore_wait(sem, 4)


def remote(src, dst, send_sem, recv_sem, target):
    return pltpu.make_async_remote_copy(
        src_ref=src, dst_ref=dst, send_sem=send_sem, recv_sem=recv_sem, device_id=target, device_id_type=MESH
    )


def span(first, count, unit):
    return pl.ds(pl.multiple_of(first, unit), count)


class RingGather:
    def __init__(self, n, parts, keep, sems):
        self.n, self.parts, self.keep = n, parts, keep
        self.send_sem, self.recv_sem = sems
        self.place, self.at = ring_place(n)

    def copy(self, way, part, step):
        sign = 1 - 2 * way
        ref = self.keep(way, part, self.at(self.place - sign * step))
        return remote(
            ref,
            ref,
            self.send_sem.at[way, part, step],
            self.recv_sem.at[way, part, step],
            {"dp": self.at(self.place + sign)},
        )

    def step(self, k):
        for part in range(self.parts):
            for way in (0, 1):
                if k > 0:
                    self.copy(way, part, k - 1).wait_recv()
                if k < self.n - 1:
                    self.copy(way, part, k).start()

    def finish(self):
        for k in range(self.n - 1):
            for part in range(self.parts):
                for way in (0, 1):
                    self.copy(way, part, k).wait_send()


class RowGather:
    def __init__(self, keep, sems):
        self.keep = keep
        self.send_sem, self.recv_sem = sems
        self.me, self.other, self.across = tensor_place()

    def copy(self, kind, part):
        ref = self.keep(part, self.across if kind == 2 else self.me)
        target = self.across if kind == 0 else self.other
        return remote(
            ref, ref, self.send_sem.at[kind, part], self.recv_sem.at[kind, part], {"tensor": target}
        )

    def start(self, part):
        self.copy(0, part).start()
        self.copy(1, part).start()

    def forward(self, part):
        self.copy(0, part).wait_recv()
        self.copy(2, part).start()

    def finish(self, parts):
        for part in range(parts):
            self.copy(1, part).wait_recv()
            self.copy(2, part).wait_recv()
            for kind in range(3):
                self.copy(kind, part).wait_send()


def gather_kernel(
    n, u_ref, g_ref, wzx_ref, wbc_ref, wout_ref, uf_ref, gf_ref, wx_ref, wz_ref, wb_ref, wo_ref,
    u_hold, wzx_hold, wbc_hold, wout_hold, own_sem, *sems,
):
    rows, width = wzx_ref.shape[1:]
    out_rows, out_cols = wout_ref.shape
    seqs, piece, _ = u_ref.shape
    dp = lax.axis_index("dp")
    me, other, _ = tensor_place()
    core = me % 2

    def keep_wide(ref):
        def keep(way, part, d):
            return ref.at[span(d * rows, rows, 16), pl.ds(way * width // 2 + part * width // 4, width // 4)]

        return keep

    def keep_out(way, part, d):
        first = way * out_rows // 2 + part * out_rows // 4
        return wo_ref.at[pl.ds(first, out_rows // 4), span(d * out_cols, out_cols, 128)]

    def keep_small(way, part, d):
        return wb_ref.at[span(d * rows + core * rows // 2 + way * rows // 4, rows // 4, 16), :]

    def keep_rows(part, t):
        ref = uf_ref if part < seqs else gf_ref
        return ref.at[part % seqs, span(t * piece, piece, 16), :]

    moves = [
        (wzx_ref.at[1], wzx_hold.at[1], wx_ref.at[span(dp * rows, rows, 16), :]),
        (wbc_ref, wbc_hold, wb_ref.at[span(dp * rows, rows, 16), :]),
    ]
    moves += [(u_ref.at[s], u_hold.at[s], keep_rows(s, me)) for s in range(seqs)]
    moves += [
        (wzx_ref.at[0], wzx_hold.at[0], wz_ref.at[span(dp * rows, rows, 16), :]),
        (wout_ref, wout_hold, wo_ref.at[:, span(dp * out_cols, out_cols, 128)]),
    ]
    moves += [(g_ref.at[s], u_hold.at[seqs + s], keep_rows(seqs + s, me)) for s in range(seqs)]
    loads = [pltpu.make_async_copy(a, b, own_sem.at[0, i]) for i, (a, b, _) in enumerate(moves)]
    stores = [pltpu.make_async_copy(b, c, own_sem.at[1, i]) for i, (_, b, c) in enumerate(moves)]
    for load in loads:
        load.start()
    greet(n)

    def settle(first, last):
        for load, store in zip(loads[first:last], stores[first:last]):
            load.wait()
            store.start()
        for store in stores[first:last]:
            store.wait()

    x_ring = RingGather(n, 2, keep_wide(wx_ref), sems[0:2])
    small = RingGather(n, 1, keep_small, sems[2:4])
    z_ring = RingGather(n, 2, keep_wide(wz_ref), sems[4:6])
    out_ring = RingGather(n, 2, keep_out, sems[6:8])
    token_rows = RowGather(keep_rows, sems[8:10])
    halves_send, halves_recv = sems[10:12]

    def half(ahead, whose):
        d = (dp + ahead) % n
        ref = wb_ref.at[span(d * rows + whose * rows // 2, rows // 2, 16), :]
        return remote(ref, ref, halves_send.at[ahead], halves_recv.at[ahead], {"tensor": other})

    settle(0, 1)
    x_ring.step(0)
    settle(1, 4)
    small.step(0)
    token_rows.start(0)
    token_rows.start(1)
    settle(4, len(moves))
    for k in range(1, n):
        x_ring.step(k)
        small.step(k)
        if k == n - 1:
            z_ring.step(0)
        if k == 4:
            token_rows.forward(0)
            token_rows.start(2)
        if k == 7:
            token_rows.forward(1)
            token_rows.start(3)
    for ahead in range(1, n):
        half(ahead, core).start()
    for k in range(1, n):
        z_ring.step(k)
        if k == n - 1:
            out_ring.step(0)
        if k == 4:
            token_rows.forward(2)
        if k == 7:
            token_rows.forward(3)
    for k in range(1, n):
        out_ring.step(k)
    for ahead in range(1, n):
        half(ahead, 1 - core).wait_recv()
        half(ahead, core).wait_send()
    for ring in (x_ring, small, z_ring, out_ring):
        ring.finish()
    token_rows.finish(2 * seqs)


def gather_all(n, u, g, w_zx, w_bc, w_out):
    seqs, piece, model = u.shape
    rows, width = w_zx.shape[1:]
    out_rows, out_cols = w_out.shape
    sem = pltpu.SemaphoreType.DMA
    ring = [sem((2, 2, n - 1))] * 2
    anywhere = pl.BlockSpec(memory_space=pl.ANY)
    whole = [
        (seqs, 4 * piece, model),
        (seqs, 4 * piece, model),
        (rows * n, width),
        (rows * n, width),
        (rows * n, w_bc.shape[1]),
        (out_rows, out_cols * n),
    ]
    return pl.pallas_call(
        functools.partial(gather_kernel, n),
        in_specs=[anywhere] * 5,
        out_specs=[anywhere] * 6,
        out_shape=[jax.ShapeDtypeStruct(shape, BF16) for shape in whole],
        scratch_shapes=[
            pltpu.VMEM((2 * seqs, piece, model), BF16),
            pltpu.VMEM(w_zx.shape, BF16),
            pltpu.VMEM(w_bc.shape, BF16),
            pltpu.VMEM(w_out.shape, BF16),
            sem((2, 4 + 2 * seqs)),
        ]
        + ring + [sem((2, 1, n - 1))] * 2 + ring + ring
        + [sem((3, 2 * seqs))] * 2 + [sem((n,))] * 2,
        compiler_params=pltpu.CompilerParams(
            collective_id=0, has_side_effects=True, vmem_limit_bytes=32 * 2**20
        ),
        name="gather_all",
    )(u, g, w_zx, w_bc, w_out)


class RingScatter:
    def __init__(self, n, term, slots, sems):
        self.n, self.term, self.slots = n, term, slots
        self.send_sem, self.recv_sem = sems
        self.place, self.at = ring_place(n)

    def copy(self, way, k):
        sign = 1 - 2 * way
        return remote(
            self.slots.at[way, k],
            self.slots.at[way, k + 1],
            self.send_sem.at[way, k],
            self.recv_sem.at[way, k],
            {"dp": self.at(self.place + sign)},
        )

    def step(self, way, k):
        value = self.term(way, self.at(self.place - (1 - 2 * way) * (1 + k)))

        @pl.when(k == 0)
        def _():
            self.slots[way, 0] = value.astype(BF16)

        @pl.when(k > 0)
        def _():
            self.copy(way, k - 1).wait_recv()

            @pl.when(k < self.n - 1)
            def _():
                self.slots[way, k] = (value + self.slots[way, k].astype(F32)).astype(BF16)

        @pl.when(k < self.n - 1)
        def _():
            self.copy(way, k).start()

        return value

    def last(self, way, value):
        return value + self.slots[way, self.n - 1].astype(F32)

    def finish(self):
        for k in range(self.n - 1):
            for way in (0, 1):
                self.copy(way, k).wait_send()


class RowScatter:
    def __init__(self, parts, term, hold, sems):
        self.parts, self.term, self.hold = parts, term, hold
        self.send_sem, self.recv_sem = sems
        self.me, self.other, self.across = tensor_place()

    def copy(self, kind, part):
        return remote(
            self.hold.at[kind, 0, part],
            self.hold.at[kind, 1, part],
            self.send_sem.at[kind, part],
            self.recv_sem.at[kind, part],
            {"tensor": self.across if kind == 1 else self.other},
        )

    def step(self, j, store):
        stage, part = j // self.parts, j % self.parts
        x, core = self.me // 2, self.me % 2
        value = self.term(2 * ((x + 1 - stage // 2) % 2) + (core + 1 - stage % 2) % 2, part)

        @pl.when(stage == 0)
        def _():
            self.hold[0, 0, part] = value.astype(BF16)
            self.copy(0, part).start()

        @pl.when(stage == 1)
        def _():
            self.copy(0, part).wait_recv()
            self.hold[1, 0, part] = (value + self.hold[0, 1, part].astype(F32)).astype(BF16)
            self.copy(1, part).start()

        @pl.when(stage == 2)
        def _():
            self.hold[2, 0, part] = value.astype(BF16)
            self.copy(2, part).start()

        @pl.when(stage == 3)
        def _():
            self.copy(2, part).wait_recv()
            store(part, value + self.hold[2, 1, part].astype(F32))

    def finish(self, store):
        for part in range(self.parts):
            self.copy(1, part).wait_recv()
            store(part, self.hold[1, 1, part].astype(F32))
            for kind in range(3):
                self.copy(kind, part).wait_send()


def product_term(a_ref, b_ref, count):
    def term(way, d):
        half = b_ref.shape[1] // 2
        return dot_tn(a_ref[:, span(d * count, count, 128)], b_ref[:, pl.ds(way * half, half)])

    return term


def out_kernel(
    n, normed_ref, g_ref, u_ref, dz_ref, wo_ref, mixed_ref, gout_ref, gz_ref, out_slots, z_slots, hold, *sems
):
    seqs, length = mixed_ref.shape[0], normed_ref.shape[0] // mixed_ref.shape[0]
    piece = mixed_ref.shape[1]
    count = g_ref.shape[1] // n
    half = gz_ref.shape[1] // 2
    greet(n)

    def mixed_term(t, part):
        return dot(normed_ref[span(part * length + t * piece, piece, 16), :], wo_ref[...])

    rows = RowScatter(seqs, mixed_term, hold, sems[0:2])
    rings = [
        RingScatter(n, product_term(g_ref, normed_ref, count), out_slots, sems[2:4]),
        RingScatter(n, product_term(u_ref, dz_ref, count), z_slots, sems[4:6]),
    ]

    def store(part, value):
        mixed_ref[part] = value

    def out_step(k, _):
        for way in (0, 1):
            value = rings[0].step(way, k)

            @pl.when(k == n - 1)
            def _():
                gout_ref[pl.ds(way * half, half), :] = rings[0].last(way, value).T

        rows.step(k, store)
        return 0

    def z_step(k, _):
        for way in (0, 1):
            value = rings[1].step(way, k)

            @pl.when(k == n - 1)
            def _():
                gz_ref[:, pl.ds(way * half, half)] = rings[1].last(way, value)

        return 0

    lax.fori_loop(0, n, out_step, 0)
    lax.fori_loop(0, n, z_step, 0)

    def add(part, value):
        mixed_ref[part] += value

    rows.finish(add)
    for ring in rings:
        ring.finish()


def scatter_out(n, piece, normed, g, u, dz, w_out):
    tokens, width = normed.shape
    model = g.shape[1]
    seqs = tokens // (4 * piece)
    count = model // n
    sem = pltpu.SemaphoreType.DMA
    vmem = pl.BlockSpec(memory_space=pltpu.VMEM)
    return pl.pallas_call(
        functools.partial(out_kernel, n),
        in_specs=[vmem] * 5,
        out_specs=[vmem] * 3,
        out_shape=[
            jax.ShapeDtypeStruct((seqs, piece, model), F32),
            jax.ShapeDtypeStruct((width, count), F32),
            jax.ShapeDtypeStruct((count, width), F32),
        ],
        scratch_shapes=[
            pltpu.VMEM((2, n, count, width // 2), BF16),
            pltpu.VMEM((2, n, count, width // 2), BF16),
            pltpu.VMEM((3, 2, seqs, piece, model), BF16),
        ]
        + [sem((3, seqs))] * 2 + [sem((2, n - 1))] * 4,
        compiler_params=pltpu.CompilerParams(
            collective_id=1, has_side_effects=True, vmem_limit_bytes=60 * 2**20
        ),
        name="scatter_out",
    )(normed, g, u, dz, w_out)


def in_kernel(
    n, u_ref, dz_ref, dx_ref, wz_ref, wx_ref, wb_ref, dbc_ref,
    din_ref, gx_ref, gb_ref,
    x_slots, b_slots, hold, bc_hold, low, pair_hold, swap, *sems,
):
    seqs, piece = din_ref.shape[:2]
    tokens, model = u_ref.shape
    length = tokens // seqs
    count = model // n
    half = gx_ref.shape[1] // 2
    me, other, across = tensor_place()
    core = me % 2
    greet(n)

    def bc_term(t, part):
        return dbc_ref[span(part * length + t * piece, piece, 16), :].astype(F32)

    def in_term(t, part):
        at = span(part * length + t * piece, piece, 16)
        return dot_nt(dz_ref[at, :], wz_ref[...]) + dot_nt(dx_ref[at, :], wx_ref[...])

    def b_term(way, d):
        cols = u_ref.shape[1] // n // 4
        total = 0.0
        for t, which in ((me, 0), (other, 1)):
            for part in range(seqs):
                a = u_ref[span(part * length + t * piece, piece, 16), span(d * count + core * count // 2, count // 2, 128)]
                total = total + dot_tn(a, low[which, part])
        return total[way * cols : (way + 1) * cols]

    bc_rows = RowScatter(seqs, bc_term, bc_hold, sems[0:2])
    in_rows = RowScatter(seqs, in_term, hold, sems[2:4])
    x_ring = RingScatter(n, product_term(u_ref, dx_ref, count), x_slots, sems[4:6])
    b_ring = RingScatter(n, b_term, b_slots, sems[6:8])
    pair_send, pair_recv, swap_send, swap_recv = sems[8:12]

    def bc_store(part, value):
        pair_hold[part] = value

    def bc_step(j, _):
        bc_rows.step(j, bc_store)
        return 0

    lax.fori_loop(0, 4 * seqs, bc_step, 0)

    def store(part, value):
        din_ref[part] = value

    def step(k, _):
        for way in (0, 1):
            value = x_ring.step(way, k)

            @pl.when(k == n - 1)
            def _():
                gx_ref[:, pl.ds(way * half, half)] = x_ring.last(way, value)

        in_rows.step(k, store)
        return 0

    lax.fori_loop(0, n, step, 0)

    def bc_add(part, value):
        low[0, part] = (pair_hold[part] + value).astype(BF16)

    bc_rows.finish(bc_add)
    pair = remote(low.at[0], low.at[1], pair_send, pair_recv, {"tensor": other})
    pair.start()
    pair.wait_recv()

    def b_step(k, _):
        for way in (0, 1):
            value = b_ring.step(way, k)

            @pl.when(k == n - 1)
            def _():
                swap[0, pl.ds(way * count // 4, count // 4), :] = b_ring.last(way, value)

        return 0

    lax.fori_loop(0, n, b_step, 0)
    cross = remote(swap.at[0], swap.at[1], swap_send.at[0], swap_recv.at[0], {"tensor": across})
    cross.start()

    def add(part, value):
        din_ref[part] += value + dot_nt(low[0, part], wb_ref[...])

    in_rows.finish(add)
    cross.wait_recv()
    swap[2] = swap[0] + swap[1]
    fold = remote(swap.at[2], swap.at[3], swap_send.at[1], swap_recv.at[1], {"tensor": other})
    fold.start()
    gb_ref[span(core * count // 2, count // 2, 16), :] = swap[2]
    fold.wait_recv()
    gb_ref[span((1 - core) * count // 2, count // 2, 16), :] = swap[3]
    pair.wait_send()
    cross.wait_send()
    fold.wait_send()
    for ring in (x_ring, b_ring):
        ring.finish()


def scatter_in(n, piece, u, dz, dx, w_z, w_x, w_bc, dbc):
    tokens, model = u.shape
    width = dz.shape[1]
    small = dbc.shape[1]
    seqs = tokens // (4 * piece)
    count = model // n
    sem = pltpu.SemaphoreType.DMA
    vmem = pl.BlockSpec(memory_space=pltpu.VMEM)
    return pl.pallas_call(
        functools.partial(in_kernel, n),
        in_specs=[vmem] * 7,
        out_specs=[vmem] * 3,
        out_shape=[
            jax.ShapeDtypeStruct((seqs, piece, model), F32),
            jax.ShapeDtypeStruct((count, width), F32),
            jax.ShapeDtypeStruct((count, small), F32),
        ],
        scratch_shapes=[
            pltpu.VMEM((2, n, count, width // 2), BF16),
            pltpu.VMEM((2, n, count // 4, small), BF16),
            pltpu.VMEM((3, 2, seqs, piece, model), BF16),
            pltpu.VMEM((3, 2, seqs, piece, small), BF16),
            pltpu.VMEM((2, seqs, piece, small), BF16),
            pltpu.VMEM((seqs, piece, small), F32),
            pltpu.VMEM((4, count // 2, small), F32),
        ]
        + [sem((3, seqs))] * 4 + [sem((2, n - 1))] * 4 + [sem(())] * 2 + [sem((2,))] * 2,
        compiler_params=pltpu.CompilerParams(
            collective_id=2, has_side_effects=True, vmem_limit_bytes=62 * 2**20
        ),
        name="scatter_in",
    )(u, dz, dx, w_z, w_x, w_bc, dbc)


def rms_scale(values):
    return lax.rsqrt(jnp.mean(values * values, axis=-1, keepdims=True) + EPS)


def gather_plain(u, g, w_zx, w_bc, w_out):
    w_zx = lax.all_gather(w_zx, "dp", axis=1, tiled=True)
    return (
        lax.all_gather(u, "tensor", axis=1, tiled=True),
        lax.all_gather(g, "tensor", axis=1, tiled=True),
        w_zx[1],
        w_zx[0],
        lax.all_gather(w_bc, "dp", axis=0, tiled=True),
        lax.all_gather(w_out, "dp", axis=1, tiled=True),
    )


def rows_of(values, piece):
    by_seq = values.reshape(-1, 4 * piece, values.shape[-1])
    return lax.psum_scatter(by_seq, "tensor", scatter_dimension=1, tiled=True)


def scatter_out_plain(piece, normed, g, u, dz, w_out):
    return (
        rows_of(dot(normed, w_out), piece),
        lax.psum_scatter(dot_tn(normed, g), "dp", scatter_dimension=1, tiled=True),
        lax.psum_scatter(dot_tn(u, dz), "dp", scatter_dimension=0, tiled=True),
    )


def scatter_in_plain(piece, u, dz, dx, w_z, w_x, w_bc, dbc):
    low = lax.psum(dbc.astype(F32), "tensor").astype(BF16)
    d_in = rows_of(dot_nt(dz, w_z) + dot_nt(dx, w_x), piece)
    first = lax.axis_index("tensor") * piece
    own = lax.dynamic_slice_in_dim(low.reshape(-1, 4 * piece, low.shape[1]), first, piece, 1)
    d_in = d_in + jnp.einsum("slc,dc->sld", own, w_bc, preferred_element_type=F32)
    return (
        d_in,
        lax.psum_scatter(dot_tn(u, dx), "dp", scatter_dimension=0, tiled=True),
        lax.psum_scatter(dot_tn(u, low), "dp", scatter_dimension=0, tiled=True),
    )


def local(
    n_dp,
    n_tensor,
    hidden,
    pre_gain,
    w_zx,
    w_bcdt,
    conv_x,
    conv_bc,
    dt_bias,
    a_log,
    d_skip,
    gate_gain,
    w_out,
    cotangent,
    segments,
):
    seqs, piece, model = hidden.shape
    length = segments.shape[1]
    tokens = seqs * length
    heads = dt_bias.shape[0]
    channels = conv_x.shape[1]
    n2 = conv_bc.shape[1]
    columns = w_bcdt.shape[1]
    tensor = lax.axis_index("tensor")
    kernels = n_dp == 8 and n_tensor == 4

    x_piece = hidden.astype(F32)
    scale_in = rms_scale(x_piece)
    u_piece = (x_piece * scale_in * pre_gain).astype(BF16)
    w_bc_piece = jnp.pad(w_bcdt, ((0, 0), (0, -columns % 128)))
    gather = functools.partial(gather_all, n_dp) if kernels else gather_plain
    u, g, w_x, w_z, w_bc, w_o = gather(u_piece, cotangent, w_zx, w_bc_piece, w_out)
    u = u.reshape(tokens, model)
    g = g.reshape(tokens, model)

    x = dot(u, w_x).reshape(seqs, length, channels)
    z = dot(u, w_z)
    bc_dt = dot(u, w_bc).reshape(seqs, length, -1)
    bc = bc_dt[:, :, :n2]
    dt = lax.dynamic_slice_in_dim(bc_dt, n2 + tensor * heads, heads, 2)

    cols = column_masks(segments)
    segrow = segments.astype(F32)[:, None, :]
    spread = jnp.asarray(spread_matrix(heads, channels), BF16)
    skip = jnp.repeat(d_skip, channels // heads)[None]
    shared = (conv_x, conv_bc, dt_bias[None], a_log[None], skip, spread)
    y, cx, cbc, states = ssd_forward(x, bc, dt, cols, segrow, shared)

    d_normed = dot_nt(g, w_o)
    sig_z = sigmoid(z)
    silu_z = z * sig_z
    y_flat = y.reshape(tokens, channels)
    gated = y_flat * silu_z
    scaled = d_normed * gate_gain
    sums = jnp.stack([jnp.sum(gated * gated, axis=1), jnp.sum(scaled * gated, axis=1)])
    sums = lax.psum(sums, "tensor") / (channels * n_tensor)
    inverse = lax.rsqrt(sums[0] + EPS)[:, None]
    normed = (gated * inverse * gate_gain).astype(BF16)
    grad_gate = jnp.sum(d_normed * gated * inverse, axis=0)
    d_gated = inverse * scaled - gated * inverse**3 * sums[1][:, None]
    dy = (d_gated * silu_z).astype(BF16)
    dz = (d_gated * y_flat * (sig_z * (1.0 + z * (1.0 - sig_z)))).astype(BF16)

    scatter = functools.partial(scatter_out, n_dp) if kernels else scatter_out_plain
    mixed, grad_out, grad_z = scatter(piece, normed, g, u, dz, w_o)
    out_hidden = (x_piece + mixed).astype(BF16)

    dx, d_bc, d_dt, gx, gbc, gh = ssd_backward(
        dy.reshape(seqs, length, channels), x, cx, bc, cbc, dt, cols, segrow, states, shared
    )
    d_dt = lax.dynamic_update_slice_in_dim(
        jnp.zeros((seqs, length, w_bc.shape[1] - n2), F32), d_dt, tensor * heads, 2
    )
    dbc = jnp.concatenate([d_bc, d_dt], axis=2).astype(BF16).reshape(tokens, -1)

    scatter = functools.partial(scatter_in, n_dp) if kernels else scatter_in_plain
    d_in, grad_x, grad_bc = scatter(piece, u, dz, dx.reshape(tokens, channels), w_z, w_x, w_bc, dbc)

    grad_pre = jnp.sum(d_in * x_piece * scale_in, axis=(0, 1))
    gain_grad = d_in * pre_gain
    d_hidden = cotangent.astype(F32) + scale_in * gain_grad - x_piece * scale_in**3 * jnp.mean(
        gain_grad * x_piece, axis=-1, keepdims=True
    )
    grad_skip = gx[5].reshape(heads, -1).sum(axis=1)
    small_dp = lax.psum((gx[:5], gh[0, :heads], gh[1, :heads], grad_skip, grad_gate), "dp")
    small_all = lax.psum((gbc[:5], grad_pre), ("dp", "tensor"))
    return (
        out_hidden,
        d_hidden,
        small_all[1],
        jnp.stack([grad_z, grad_x]),
        grad_bc[:, :columns],
        small_dp[0],
        small_all[0],
        small_dp[1],
        small_dp[2],
        small_dp[3],
        small_dp[4],
        grad_out,
    )


def solution(mesh):
    placed = (
        P("dp", "tensor", None),
        P(),
        P(None, "dp", "tensor"),
        P("dp", None),
        P(None, "tensor"),
        P(),
        P("tensor"),
        P("tensor"),
        P("tensor"),
        P("tensor"),
        P("tensor", "dp"),
        P("dp", "tensor", None),
        P("dp", None),
    )
    return jax.shard_map(
        functools.partial(local, mesh.shape["dp"], mesh.shape["tensor"]),
        mesh=mesh,
        in_specs=placed,
        out_specs=(
            P("dp", "tensor", None),
            P("dp", "tensor", None),
            P(),
            P(None, "dp", "tensor"),
            P("dp", None),
            P(None, "tensor"),
            P(),
            P("tensor"),
            P("tensor"),
            P("tensor"),
            P("tensor"),
            P("tensor", "dp"),
        ),
        check_vma=False,
    )
```

time: 1680 us -> 668 us (0.40)
  waiting for transfers between devices: 699 us -> 0 us
  Pallas kernels: 0 us -> 445 us
  matrix products: 401 us -> 58.3 us
  other arithmetic: 203 us -> 35.9 us
  local copies, waits for them, and re-layouts: 189 us -> 30.9 us
  blocking collectives: 164 us -> 88.9 us
    pallas_call x0 -> x5, Pallas kernels: none -> 445 us  [the longest x1 136 us: gather_all(): pl.pallas_call(functools.partial(gather_kernel, n), in_specs=[anywhere] *...]
    reduce_scatter x7 -> x0, waiting for transfers between devices: 409 us -> none  [the longest x1 185 us: local(): lax.psum_scatter(grad_zx, 'dp', scatter_dimension=1, tiled=True)]
    dot_general x42 -> x4, matrix products: 401 us -> 58.3 us  [the longest x3 44.9 us: dot(): return jnp.dot(a, b, preferred_element_type=F32)]
    all_gather x7 -> x0, waiting for transfers between devices: 287 us -> none  [the longest x1 115 us: local(): lax.all_gather(w_zx, 'dp', axis=1, tiled=True)]
    reshape x39 -> x2, local copies, waits for them, and re-layouts: 121 us -> 0.04 us  [the longest x1 0.02 us: column_masks(): jnp.pad(segments, ((0, 0), (1, 0)), constant_values=-1)[:, :length]]
    reduce_sum x20 -> x2, other arithmetic: 85.4 us -> 3.71 us  [the longest x1 3.59 us: local(): grad_pre = jnp.sum(d_in * x_piece * scale_in, axis=(0, 1))]
    psum x5 -> x3, blocking collectives: 164 us -> 88.9 us  [the longest x1 41.8 us: local(): small_all = lax.psum((gbc[:5], grad_pre), ('dp', 'tensor'))]
    another operation x15 -> x4, other arithmetic: 36.1 us -> 3.16 us  [the longest x1 2.94 us: local(): jnp.stack([grad_z, grad_x])]
  transfers between devices with their start and end apart: 14 -> 0, of which waited for: 8 -> 0; matrix products, arithmetic and copies ran while one was open for 32% -> 0% of each run, Pallas kernels for 0% -> 0%
where the time goes in v1:
time: 668 us; the launch traced here: 660 us
  Pallas kernels  445 us (67%)
  blocking collectives  88.9 us (13%)
  matrix products  58.3 us (9%)
  other arithmetic  35.9 us (5%)
  local copies, waits for them, and re-layouts  30.9 us (5%)
    pallas_call x1, Pallas kernels, gather_all(): pl.pallas_call(functools.partial(gather_kernel, n), in_specs=[anywhere] *...  136 us
    pallas_call x1, Pallas kernels, scatter_out(): pl.pallas_call(functools.partial(out_kernel, n), in_specs=[vmem] * 5, out...  118 us
    pallas_call x1, Pallas kernels, scatter_in(): pl.pallas_call(functools.partial(in_kernel, n), in_specs=[vmem] * 7, out_...  104 us
    pallas_call x1, Pallas kernels, ssd_backward(): pl.pallas_call(backward_kernel, grid=(seqs, blocks), in_specs=[tok(channe...  61.1 us
    dot_general x3, matrix products, dot(): return jnp.dot(a, b, preferred_element_type=F32)  44.9 us
    psum x1, blocking collectives, local(): small_all = lax.psum((gbc[:5], grad_pre), ('dp', 'tensor'))  41.8 us
    psum x1, blocking collectives, local(): lax.psum((gx[:5], gh[0, :heads], gh[1, :heads], grad_skip, grad_gate), 'dp')  36.5 us
    pallas_call x1, Pallas kernels, ssd_forward(): pl.pallas_call(forward_kernel, grid=(seqs, blocks), in_specs=[tok(channel...  26 us

profile of v1, /device:TPU:0, one launch (start us, length us, event | category | flops | bytes accessed | tf_op | source)
XLA Modules:
  0.0 660.2 jit_solution(14542705748024716282)
XLA Ops:
  0.7 2.2 fusion.3
  2.9 3.5 fusion.5.u_ref
  6.4 0.2 copy.59
  6.6 1.6 copy-done.4
  8.2 1.0 copy-done.14
  9.2 135.9 %gather_all.1 = (bf16[2,1024,2048]{2,1,0:T(8,128)(2,1)}, bf16[2,1024,2048]{2,1,0:T(8,128)(2,1)}, bf16[2048,1024]{1,0:T(8,128)(2,1)S(1)}, bf16[2048,1024]{1,0:T(8...) custom-call(bf16[2,256,2048]{2,1,0:T(8,128)(2,1)S(1)} %copy-done.4, ...), custom_call_target="tpu_custom_call" | custom-call | tf_op jit(solution)/shard_map/gather_all/pallas_call | solution.py:612
  145.2 12.3 %fusion.14 = f32[2,1024,384]{2,1,0:T(8,128)} fusion(bf16[2,1024,2048]{2,1,0:T(8,128)(2,1)} %get-tuple-element.34, bf16[2048,384]{1,0:T(8,128)(2,1)S(1)} %get-tuple-element.36.wb_ref), kind=kOutput, calls=%fused_computation.31 | convolution fusion | flops 3221225472 | bytes 13107200 | tf_op jit(solution)/shard_map/dot_general | solution.py:34
  157.5 1.6 constant_dynamic-slice_fusion.dt_ref
  159.0 0.1 fusion.23
  159.2 0.1 copy.72
  159.3 0.1 broadcast_bitcast_fusion.1
  159.4 0.1 slice.59
  159.4 0.1 copy.73
  159.5 0.1 broadcast_bitcast_fusion
  159.6 0.1 fusion.20
  159.7 0.4 copy.64
  160.1 1.4 copy.65
  161.4 1.3 copy.66
  162.8 1.3 copy.67
  164.1 1.4 copy.68
  165.5 1.4 copy.69
  166.9 1.1 stack.68
  168.0 4.4 stack.69.cols_ref
  172.4 3.5 slice.57.bc_ref
  175.9 13.2 %fusion.12.x_ref = f32[2,1024,1024]{2,1,0:T(8,128)} fusion(bf16[2,1024,2048]{2,1,0:T(8,128)(2,1)} %get-tuple-element.34, bf16[2048,1024]{1,0:T(8,128)(2,1)S(1)} %copy-done.6), kind=kOutput, calls=%fused_computation.27 | convolution fusion | flops 8589934592 | bytes 20971520 | tf_op jit(solution)/shard_map/dot_general | solution.py:34
  189.2 0.1 broadcast_in_dim_reshape.3.skip_ref
  189.4 26.0 %ssd_forward.1 = (f32[2,1024,1024]{2,1,0:T(8,128)}, f32[2,1024,1024]{2,1,0:T(8,128)}, f32[2,1024,256]{2,1,0:T(8,128)S(1)}, bf16[2,4,128,1024]{3,2,1,0:T(8,128)(2,1)}) custom-call(f32[2,1024,1024]{2,1,0:T(8,128)} %fusion.12.x_ref, f32[2,1024,256]{2,1,0:T(8,128)} %slice.57.bc_ref, f32[2,1024,16]{2,1,0:T(8,128)S(1)} %constant_dynamic-slice_fusion.dt_ref, ...), custom_call_target="tpu_custom_call" | custom-call | tf_op jit(solution)/shard_map/ssd_forward/pallas_call | solution.py:340
  215.4 1.4 copy-done.11
  216.8 13.3 %fusion.24 = f32[2048,1024]{1,0:T(8,128)} fusion(bf16[2048,2048]{1,0:T(8,128)(2,1)} %bitcast.80, bf16[1024,2048]{1,0:T(8,128)(2,1)S(1)} %copy-done.10), kind=kOutput, calls=%fused_computation.63 | convolution fusion | flops 8589934592 | bytes 20971520 | tf_op jit(solution)/shard_map/dot_general | solution.py:38
  230.1 19.4 %multiply_reduce_fusion.2 = (f32[2048]{0:T(1024)S(1)}, f32[2048]{0:T(1024)S(1)}, f32[2048,1024]{1,0:T(8,128)}) fusion(f32[2,1024,1024]{2,1,0:T(8,128)} %get-tuple-element.37, f32[2048,1024]{1,0:T(8,128)} %fusion.24, f32[1024]{0:T(1024)S(1)} %copy-done.31, bf16[2048,2048]{1,0:T(8,128)(2,1)} %bitcast.76, bf16[2048,1024]{1,0:T(8,128)(2,1)S(1)} %copy-done.8), kind=kOutput, calls=%fused_computation.15 | convolution fusion | flops 8610902016 | bytes 37769216 | tf_op jit(solution)/shard_map/dot_general | solution.py:34
  249.6 10.6 %psum.56 = f32[2,2048]{1,0:T(2,128)S(1)} all-reduce(f32[2,2048]{1,0:T(2,128)S(1)} %pad_maximum_fusion.2), channel_id=1, replica_groups=mesh['dp'=8,'tensor'=4] {'tensor'}, use_global_device_ids=true, to_apply=%region_3.4 | all-reduce | flops 4096 | bytes 32768 | tf_op jit(solution)/shard_map/psum | solution.py:1051
  260.3 15.3 %multiply_convert_fusion = (bf16[2048,1024]{1,0:T(8,128)(2,1)}, bf16[2048,1024]{1,0:T(8,128)(2,1)}, f32[1024]{0:T(1024)S(1)}, bf16[2048,1024]{1,0:T(8,128)(2,1)}) fusion(f32[2048,1024]{1,0:T(8,128)} %get-tuple-element.135, f32[2048]{0:T(1024)S(1)} %bitcast.93, f32[2048,1024]{1,0:T(8,128)} %fusion.24, f32[2048]{0:T(1024)S(1)} %multiply_multiply_fusion, ...), kind=kLoop, calls=%fused_computation.11 | loop fusion | flops 52427776 | bytes 37781504 | tf_op jit(solution)/shard_map/convert_element_type | solution.py:1056
  275.6 61.1 %ssd_backward.1 = (bf16[2,1024,1024]{2,1,0:T(8,128)(2,1)}, f32[2,1024,256]{2,1,0:T(8,128)}, f32[2,1024,16]{2,1,0:T(8,128)}, f32[8,1024]{1,0:T(8,128)}, f32[8,256]{1,0:T(8,128)}, /*index=5*/f32[8,128]{1,0:T(8,128)}) custom-call(bf16[2,1024,1024]{2,1,0:T(8,128)(2,1)} %bitcast.79, f32[2,1024,1024]{2,1,0:T(8,128)} %fusion.12.x_ref, ...), custom_call_target="tpu_custom_call" | custom-call | tf_op jit(solution)/shard_map/ssd_backward/pallas_call | solution.py:370
  336.7 0.8 slice_reduce_fusion
  337.5 0.1 reduce_sum.68
  337.7 0.8 slice_bitcast_fusion
  338.4 36.5 %all-reduce.5 = (f32[5,1024]{1,0:T(8,128)}, f32[16]{0:T(128)}, f32[16]{0:T(128)}, f32[16]{0:T(128)}, f32[1024]{0:T(1024)}) all-reduce(f32[5,1024]{1,0:T(8,128)} %bitcast.90, f32[16]{0:T(128)S(1)} %get-tuple-element.132, f32[16]{0:T(128)S(1)} %get-tuple-element.131, f32[16]{0:T(128)S(1)} %reduce_sum.68, ...), channel_id=1, replica_groups=mesh['dp'=8,'tensor'=4] {'dp'}, use_global_device_ids=true, to_apply=%region_7.8 | all-reduce | flops 6192 | bytes 49536 | tf_op jit(solution)/shard_map/psum | solution.py:1080
  374.9 117.8 %scatter_out.1 = (f32[2,256,2048]{2,1,0:T(8,128)}, f32[1024,256]{1,0:T(8,128)}, f32[256,1024]{1,0:T(8,128)}) custom-call(bf16[2048,1024]{1,0:T(8,128)(2,1)} %get-tuple-element.118.normed_ref, bf16[2048,2048]{1,0:T(8,128)(2,1)} %bitcast.81, bf16[2048,2048]{1,0:T(8,128)(2,1)} %bitcast.77, bf16[2048,1024]{1,0:T(8,128)(2,1)} %get-tuple-element.116.dz_ref, ...), custom_call_target="tpu_custom_call" | custom-call | tf_op jit(solution)/shard_map/scatter_out/pallas_call | solution.py:796
  492.7 4.8 dynamic_update_slice.3
  497.6 0.1 convert.13
  497.7 1.3 pad_maximum_fusion.1.dbc_ref
  499.0 104.0 %scatter_in.1 = (f32[2,256,2048]{2,1,0:T(8,128)}, f32[256,1024]{1,0:T(8,128)}, f32[256,384]{1,0:T(8,128)}) custom-call(bf16[2048,2048]{1,0:T(8,128)(2,1)} %bitcast.78, bf16[2048,1024]{1,0:T(8,128)(2,1)} %get-tuple-element.116.dz_ref, bf16[2048,1024]{1,0:T(8,128)(2,1)} %bitcast.82, bf16[2048,1024]{1,0:T(8,128)(2,1)} %copy-done.7, ...), custom_call_target="tpu_custom_call" | custom-call | tf_op jit(solution)/shard_map/scatter_in/pallas_call | solution.py:927
  603.1 2.9 pad_maximum_fusion
  606.0 3.6 fusion.11
  609.6 41.8 %all-reduce.4 = (f32[2048]{0:T(1024)}, f32[5,256]{1,0:T(8,128)}) all-reduce(f32[2048]{0:T(1024)S(1)} %get-tuple-element.106, f32[5,256]{1,0:T(8,128)S(1)} %bitcast.94), channel_id=1, replica_groups=mesh['dp'=8,'tensor'=4] {'dp','tensor'}, use_global_device_ids=true, to_apply=%region_6.7 | all-reduce | flops 3328 | bytes 26624 | tf_op jit(solution)/shard_map/psum | solution.py:1081
  651.5 6.6 %fusion.8 = (f32[2,256,2048]{2,1,0:T(8,128)}, bf16[2,256,2048]{2,1,0:T(8,128)(2,1)}) fusion(bf16[2,256,2048]{2,1,0:T(8,128)(2,1)} %param.14, bf16[2,256,2048]{2,1,0:T(8,128)(2,1)S(1)} %copy-done.3, f32[2,256,2048]{2,1,0:T(8,128)} %get-tuple-element.48, f32[2,256]{1,0:T(2,128)S(1)} %broadcast_multiply_fusion.1, f32[2,256]{1,0:T(2,128)S(1)} %get-tuple-element.133, ...), kind=kLoop, calls=%fused_computation.23 | loop fusion | flops 10485760 | bytes 18888704 | tf_op jit(solution)/shard_map/sub | solution.py:1076
  658.1 0.9 copy.70
  658.9 1.0 copy.78
  (79 shorter events, 0.5 us)
Async XLA Ops:
  0.6 5.7 copy-start.27
  0.7 5.9 copy-start.13
  0.7 5.9 copy-start.2
  6.6 1.6 copy-start.4
  8.2 1.0 copy-start.14
  145.1 12.3 %copy-start.5 = (bf16[2048,1024]{1,0:T(8,128)(2,1)}, bf16[2048,1024]{1,0:T(8,128)(2,1)S(1)}, u32[]{:S(2)}) copy-start(bf16[2048,1024]{1,0:T(8,128)(2,1)S(1)} %get-tuple-element.35.wx_ref) | copy-start | bytes 12582916
  145.1 12.3 %copy-start.7 = (bf16[2048,1024]{1,0:T(8,128)(2,1)}, bf16[2048,1024]{1,0:T(8,128)(2,1)S(1)}, u32[]{:S(2)}) copy-start(bf16[2048,1024]{1,0:T(8,128)(2,1)S(1)} %get-tuple-element.38.wz_ref) | copy-start | bytes 12582916
  145.2 12.3 %copy-start.9 = (bf16[1024,2048]{1,0:T(8,128)(2,1)}, bf16[1024,2048]{1,0:T(8,128)(2,1)S(1)}, u32[]{:S(2)}) copy-start(bf16[1024,2048]{1,0:T(8,128)(2,1)S(1)} %get-tuple-element.40.wo_ref) | copy-start | bytes 12582916
  145.2 12.3 %copy-start.12 = (bf16[2048,384]{1,0:T(8,128)(2,1)}, bf16[2048,384]{1,0:T(8,128)(2,1)S(1)}, u32[]{:S(2)}) copy-start(bf16[2048,384]{1,0:T(8,128)(2,1)S(1)} %get-tuple-element.36.wb_ref) | copy-start | bytes 4718596
  145.2 13.9 %copy-start.29 = (s32[2,1024]{1,0:T(2,128)S(1)}, s32[2,1024]{1,0:T(2,128)}, u32[]{:S(2)}) copy-start(s32[2,1024]{1,0:T(2,128)} %param.26) | copy-start | bytes 24580
  159.0 30.3 %copy-start = (f32[2,1024,16]{2,1,0:T(8,128)}, f32[2,1024,16]{2,1,0:T(8,128)S(1)}, u32[]{:S(2)}) copy-start(f32[2,1024,16]{2,1,0:T(8,128)S(1)} %constant_dynamic-slice_fusion.dt_ref) | copy-start | bytes 393220
  172.3 17.0 %copy-start.1 = (f32[2,1024,8]{2,1,0:T(8,128)}, f32[2,1024,8]{2,1,0:T(8,128)S(1)}, u32[]{:S(2)}) copy-start(f32[2,1024,8]{2,1,0:T(8,128)S(1)} %stack.69.cols_ref) | copy-start | bytes 196612
  172.3 3.5 copy-start.6
  175.8 13.3 %copy-start.32 = (f32[16]{0:T(128)S(1)}, f32[16]{0:T(128)}, u32[]{:S(2)}) copy-start(f32[16]{0:T(128)} %param.22) | copy-start | bytes 196
  175.8 13.5 %copy-start.15 = (f32[5,1024]{1,0:T(8,128)S(1)}, f32[5,1024]{1,0:T(8,128)}, u32[]{:S(2)}) copy-start(f32[5,1024]{1,0:T(8,128)} %taps_x_ref.3) | copy-start | bytes 61444
  175.8 13.5 %copy-start.16 = (bf16[16,1024]{1,0:T(8,128)(2,1)S(1)}, bf16[16,1024]{1,0:T(8,128)(2,1)}, u32[]{:S(2)}) copy-start(bf16[16,1024]{1,0:T(8,128)(2,1)} %constant.39.clone.spread_ref) | copy-start | bytes 98308
  175.8 13.5 %copy-start.19 = (f32[5,256]{1,0:T(8,128)S(1)}, f32[5,256]{1,0:T(8,128)}, u32[]{:S(2)}) copy-start(f32[5,256]{1,0:T(8,128)} %taps_bc_ref.3) | copy-start | bytes 15364
  175.8 13.5 %copy-start.20 = (f32[16]{0:T(128)S(1)}, f32[16]{0:T(128)}, u32[]{:S(2)}) copy-start(f32[16]{0:T(128)} %param.20) | copy-start | bytes 196
  175.9 13.5 %copy-start.21 = (f32[16]{0:T(128)S(1)}, f32[16]{0:T(128)}, u32[]{:S(2)}) copy-start(f32[16]{0:T(128)} %param.21) | copy-start | bytes 196
  189.1 26.2 %copy-start.17 = (f32[2,1,1024]{2,1,0:T(1,128)}, f32[2,1,1024]{2,1,0:T(1,128)S(1)}, u32[]{:S(2)}) copy-start(f32[2,1,1024]{2,1,0:T(1,128)S(1)} %broadcast_in_dim.10.segrow_ref) | copy-start | bytes 24580
  189.3 26.1 %copy-start.18 = (f32[1,1024]{1,0:T(1,128)}, f32[1,1024]{1,0:T(1,128)S(1)}, u32[]{:S(2)}) copy-start(f32[1,1024]{1,0:T(1,128)S(1)} %broadcast_in_dim_reshape.3.skip_ref) | copy-start | bytes 12292
  189.4 27.4 %copy-start.10 = (bf16[1024,2048]{1,0:T(8,128)(2,1)S(1)}, bf16[1024,2048]{1,0:T(8,128)(2,1)}, u32[]{:S(2)}) copy-start(bf16[1024,2048]{1,0:T(8,128)(2,1)} %copy-done.9) | copy-start | bytes 12582916
  215.4 1.4 copy-start.11
  216.8 13.4 %copy-start.8 = (bf16[2048,1024]{1,0:T(8,128)(2,1)S(1)}, bf16[2048,1024]{1,0:T(8,128)(2,1)}, u32[]{:S(2)}) copy-start(bf16[2048,1024]{1,0:T(8,128)(2,1)} %copy-done.7) | copy-start | bytes 12582916
  216.8 13.4 %copy-start.31 = (f32[1024]{0:T(1024)S(1)}, f32[1024]{0:T(1024)}, u32[]{:S(2)}) copy-start(f32[1024]{0:T(1024)} %param.23) | copy-start | bytes 12292
  374.9 122.7 %copy-start.23 = (f32[2,1024,256]{2,1,0:T(8,128)S(1)}, f32[2,1024,256]{2,1,0:T(8,128)}, u32[]{:S(2)}) copy-start(f32[2,1024,256]{2,1,0:T(8,128)} %get-tuple-element.46) | copy-start | bytes 6291460
  499.0 104.1 %copy-start.25 = (f32[256,1024]{1,0:T(8,128)S(1)}, f32[256,1024]{1,0:T(8,128)}, u32[]{:S(2)}) copy-start(f32[256,1024]{1,0:T(8,128)} %get-tuple-element.49) | copy-start | bytes 3145732
  603.0 3.0 copy-start.22
  603.0 3.0 copy-start.28
  606.0 3.6 copy-start.30
  606.0 45.4 %copy-start.3 = (bf16[2,256,2048]{2,1,0:T(8,128)(2,1)S(1)}, bf16[2,256,2048]{2,1,0:T(8,128)(2,1)}, u32[]{:S(2)}) copy-start(bf16[2,256,2048]{2,1,0:T(8,128)(2,1)} %g_ref.1) | copy-start | bytes 6291460
  651.4 6.6 %copy-start.26 = (f32[256,384]{1,0:T(8,128)S(1)}, f32[256,384]{1,0:T(8,128)}, u32[]{:S(2)}) copy-start(f32[256,384]{1,0:T(8,128)} %get-tuple-element.51) | copy-start | bytes 1179652
  651.4 7.5 %copy-start.24 = (f32[1024,256]{1,0:T(8,128)S(1)}, f32[1024,256]{1,0:T(8,128)}, u32[]{:S(2)}) copy-start(f32[1024,256]{1,0:T(8,128)} %get-tuple-element.159) | copy-start | bytes 3145732

commit v2 on v1

--- a/solution.py
+++ b/solution.py
@@ -158,13 +158,12 @@
     state[...] = carry_e * state[...] + dot_tn(b_mat, scaled)
 
 
-def backward_kernel(
-    dy_ref, x_ref, cx_ref, bc_ref, cbc_ref, dt_ref, cols_ref, segrow_ref, states_ref,
+def backward_block(
+    seq, step_id, dy_ref, x_ref, cx_ref, bc_ref, cbc_ref, dt_ref, cols_ref, segrow_ref, states_ref,
     taps_x_ref, taps_bc_ref, bias_ref, alog_ref, skip_ref, spread_ref,
-    dx_ref, dbc_ref, ddt_ref, gx_ref, gbc_ref, gh_ref,
+    dx_ref, dbc_ref, gx_ref, gbc_ref, gh_ref,
     ds_x, ds_bc, d_state, mask_bias, d_scores, d_in, row_sums,
 ):
-    seq, step_id = pl.program_id(0), pl.program_id(1)
     q = BLOCK
     heads = dt_ref.shape[-1]
     channels = x_ref.shape[-1]
@@ -172,8 +171,8 @@
 
     @pl.when(step_id == 0)
     def _():
-        ds_x[:, q : q + 8, :] = jnp.zeros((4, 8, channels), F32)
-        ds_bc[:, q : q + 8, :] = jnp.zeros((4, 8, ds_bc.shape[2]), F32)
+        ds_x[:, q : q + 8, :] = jnp.zeros((3, 8, channels), F32)
+        ds_bc[:, q : q + 8, :] = jnp.zeros((3, 8, ds_bc.shape[2]), F32)
         d_state[...] = jnp.zeros_like(d_state)
 
     @pl.when((step_id == 0) & (seq == 0))
@@ -193,18 +192,12 @@
     scores = exact_nt(bc[:, :n], bc[:, n:])
     b_mat, c_mat = bc[:, :n].astype(BF16), bc[:, n:].astype(BF16)
     cx = cx_ref[0]
-    sig_x = sigmoid(cx)
-    xc = cx * sig_x
-    xb = xc.astype(BF16)
-    xbf = xb.astype(F32)
+    xb = (cx * sigmoid(cx)).astype(BF16)
     dyb = dy_ref[0]
-    dyf = dyb.astype(F32)
 
     biased, step, rate, cum = head_sizes(dt_ref[0], bias_ref[...], alog_ref[...])
     cum_end = cum[q - 1 : q, :]
     spread = spread_ref[...]
-    reads_e = expand(reads * jnp.exp2(cum), spread)
-    to_end_e = expand(last * jnp.exp2(cum_end - cum) * step, spread)
     carry_e = expand(jnp.broadcast_to(jnp.exp2(cum_end), (8, heads)), spread)[0:1]
     source = cum - jnp.log(step) * LOG2E
     target = transpose_heads(cum)
@@ -215,14 +208,17 @@
 
     st = states_ref[0, 0]
     dst = d_state[...].astype(BF16)
-    dye = (dyf * reads_e).astype(BF16)
-    scaled = (xbf * to_end_e).astype(BF16)
+    dye = dyb.astype(F32) * expand(reads * jnp.exp2(cum), spread)
+    out_h = gather_heads(dye * dot(c_mat, st), spread)
+    dye = dye.astype(BF16)
     d_c = dot_nt(dye, st)
-    d_b = dot_nt(scaled, dst)
+    carried = carry_e * jnp.sum(d_state[...] * st.astype(F32), axis=0, keepdims=True)
+    d_state[...] = carry_e * d_state[...] + dot_tn(c_mat, dye)
+    to_end_e = expand(last * jnp.exp2(cum_end - cum) * step, spread)
+    d_b = dot_nt((xb.astype(F32) * to_end_e).astype(BF16), dst)
     dx_st = dot(b_mat, dst) * to_end_e
-    carried = carry_e * jnp.sum(d_state[...] * st.astype(F32), axis=0, keepdims=True)
-    out_part = dyf * reads_e * dot(c_mat, st)
-    d_state[...] = carry_e * d_state[...] + dot_tn(c_mat, dye)
+    state_h = gather_heads(xb.astype(F32) * dx_st, spread)
+    d_in[...] = dx_st
 
     half = q // 2
     lane = lax.broadcasted_iota(jnp.int32, (1, 2 * width), 1)
@@ -261,17 +257,14 @@
             top = (top * scores[:half, :]).astype(BF16)
             low = (low * scores[half:, half:]).astype(BF16)
             both.append(jnp.concatenate([dot(top, dyp), dot(low, dyp[half:])], axis=0))
-        d_in[:, at] = jnp.where(lane < width, both[0], both[1])
+        d_in[:, at] += jnp.where(lane < width, both[0], both[1])
 
     dsb = d_scores[...].astype(BF16)
     d_b = d_b + dot(dsb, c_mat)
     d_c = d_c + dot_tn(dsb, b_mat)
 
-    dx = d_in[...] + dx_st
-    skip = skip_ref[...]
-    state_h = gather_heads(xbf * dx_st, spread)
     used_h = col_sums + state_h
-    diff_h = row_sums[...].T[:, :heads] - col_sums + gather_heads(out_part, spread)
+    diff_h = row_sums[...].T[:, :heads] - col_sums + out_h
     from_here = (rows <= places).astype(F32)
     before = (rows > places).astype(F32)
     d_rate = (
@@ -282,27 +275,33 @@
     sig_dt = sigmoid(biased)
     ratio = jnp.where(step < 1e-30, 1.0, sig_dt / jnp.maximum(step, 1e-30))
     d_raw = used_h * ratio - jnp.exp(alog_ref[...]) * sig_dt * d_rate
-    ddt_ref[0] = d_raw
+    lanes = dbc_ref.shape[2] - 2 * n
+    mine = lax.broadcasted_iota(jnp.int32, (heads, lanes), 0) + lax.axis_index("tensor") * heads
+    own = (lax.broadcasted_iota(jnp.int32, (heads, lanes), 1) == mine).astype(BF16)
+    dbc_ref[0, :, 2 * n :] = dot(d_raw.astype(BF16), own).astype(BF16)
     gh_ref[0:1, :heads] += jnp.sum(d_raw, axis=0, keepdims=True)
     gh_ref[1:2, :heads] += jnp.sum(d_rate * rate, axis=0, keepdims=True)
 
     def conv_back(d_out, value_ref, hold, taps_ref, grad_ref):
-        value = value_ref[0]
+        value = value_ref[0].astype(F32)
         d_value = d_out * taps_ref[3:4, :]
         grad_ref[3:4, :] += jnp.sum(value * d_out, axis=0, keepdims=True)
         grad_ref[4:5, :] += jnp.sum(d_out, axis=0, keepdims=True)
         for lag in (1, 2, 3):
-            hold[lag, 0:q, :] = lag_masks[lag - 1] * d_out
-            moved = hold[lag, lag : lag + q, :]
+            hold[lag - 1, 0:q, :] = lag_masks[lag - 1] * d_out
+            moved = hold[lag - 1, lag : lag + q, :]
             d_value = d_value + moved * taps_ref[3 - lag : 4 - lag, :]
             grad_ref[3 - lag : 4 - lag, :] += jnp.sum(value * moved, axis=0, keepdims=True)
-            hold[lag, q : q + 8, :] = hold[lag, 0:8, :]
+            hold[lag - 1, q : q + 8, :] = hold[lag - 1, 0:8, :]
         return d_value
 
     d_bc = jnp.concatenate([d_b, d_c], axis=1) * (sig_bc * (1.0 + cbc * (1.0 - sig_bc)))
-    dbc_ref[0] = conv_back(d_bc, bc_ref, ds_bc, taps_bc_ref, gbc_ref)
-    gx_ref[5:6, :] += jnp.sum(dyf * xbf, axis=0, keepdims=True)
-    d_cx = (dx + skip * dyf) * (sig_x * (1.0 + cx * (1.0 - sig_x)))
+    dbc_ref[0, :, : 2 * n] = conv_back(d_bc, bc_ref, ds_bc, taps_bc_ref, gbc_ref).astype(BF16)
+    dyf = dy_ref[0].astype(F32)
+    cx = cx_ref[0]
+    sig_x = sigmoid(cx)
+    gx_ref[5:6, :] += jnp.sum(dyf * (cx * sig_x).astype(BF16).astype(F32), axis=0, keepdims=True)
+    d_cx = (d_in[...] + skip_ref[...] * dyf) * (sig_x * (1.0 + cx * (1.0 - sig_x)))
     dx_ref[0] = conv_back(d_cx, x_ref, ds_x, taps_x_ref, gx_ref).astype(BF16)
 
 
@@ -361,37 +360,62 @@
     )(x, bc, dt, cols, segrow, *shared)
 
 
-def ssd_backward(dy, x, cx, bc, cbc, dt, cols, segrow, states, shared):
+def backward_kernel(*refs):
+    backward_block(pl.program_id(0), pl.program_id(1), *refs)
+
+
+def backward_scratch(channels, n2):
+    return [
+        pltpu.VMEM((3, BLOCK + 8, channels), F32),
+        pltpu.VMEM((3, BLOCK + 8, n2), F32),
+        pltpu.VMEM((n2 // 2, channels), F32),
+        pltpu.VMEM((BLOCK, BLOCK), F32),
+        pltpu.VMEM((BLOCK, BLOCK), F32),
+        pltpu.VMEM((BLOCK, channels), F32),
+        pltpu.VMEM((128, BLOCK), F32),
+    ]
+
+
+def backward_specs(channels, n2, heads, small, place):
+    tok = lambda w: pl.BlockSpec((1, BLOCK, w), lambda *i: (*place(*i), 0))
+    full = lambda *shape: pl.BlockSpec(shape, lambda *i: (0,) * len(shape))
+    ins = [tok(channels)] * 3 + [tok(n2)] * 2 + [
+        tok(heads),
+        tok(8),
+        pl.BlockSpec((1, 1, BLOCK), lambda *i: (place(*i)[0], 0, place(*i)[1])),
+        pl.BlockSpec((1, 1, n2 // 2, channels), lambda *i: (*place(*i), 0, 0)),
+        full(5, channels),
+        full(5, n2),
+        full(1, heads),
+        full(1, heads),
+        full(1, channels),
+        full(heads, channels),
+    ]
+    return ins, [tok(channels), tok(small), full(8, channels), full(8, n2), full(8, 128)]
+
+
+def backward_outs(seqs, length, channels, n2, small):
+    return [
+        jax.ShapeDtypeStruct((seqs, length, channels), BF16),
+        jax.ShapeDtypeStruct((seqs, length, small), BF16),
+        jax.ShapeDtypeStruct((8, channels), F32),
+        jax.ShapeDtypeStruct((8, n2), F32),
+        jax.ShapeDtypeStruct((8, 128), F32),
+    ]
+
+
+def ssd_backward(small, dy, x, cx, bc, cbc, dt, cols, segrow, states, shared):
     seqs, length, channels = x.shape
     n2, heads = bc.shape[2], dt.shape[2]
     blocks = length // BLOCK
-    tok = lambda w: pl.BlockSpec((1, BLOCK, w), lambda s, c: (s, blocks - 1 - c, 0))
-    whole = lambda *shape: pl.BlockSpec(shape, lambda s, c: (0,) * len(shape))
+    ins, outs = backward_specs(channels, n2, heads, small, lambda s, c: (s, blocks - 1 - c))
     return pl.pallas_call(
         backward_kernel,
         grid=(seqs, blocks),
-        in_specs=[tok(channels)] * 3 + [tok(n2)] * 2 + [tok(heads), tok(8),
-                  pl.BlockSpec((1, 1, BLOCK), lambda s, c: (s, 0, blocks - 1 - c)),
-                  pl.BlockSpec((1, 1, n2 // 2, channels), lambda s, c: (s, blocks - 1 - c, 0, 0))]
-        + shared_specs(channels, n2, heads),
-        out_specs=[tok(channels), tok(n2), tok(heads), whole(8, channels), whole(8, n2), whole(8, 128)],
-        out_shape=[
-            jax.ShapeDtypeStruct((seqs, length, channels), BF16),
-            jax.ShapeDtypeStruct((seqs, length, n2), F32),
-            jax.ShapeDtypeStruct((seqs, length, heads), F32),
-            jax.ShapeDtypeStruct((8, channels), F32),
-            jax.ShapeDtypeStruct((8, n2), F32),
-            jax.ShapeDtypeStruct((8, 128), F32),
-        ],
-        scratch_shapes=[
-            pltpu.VMEM((4, BLOCK + 8, channels), F32),
-            pltpu.VMEM((4, BLOCK + 8, n2), F32),
-            pltpu.VMEM((n2 // 2, channels), F32),
-            pltpu.VMEM((BLOCK, BLOCK), F32),
-            pltpu.VMEM((BLOCK, BLOCK), F32),
-            pltpu.VMEM((BLOCK, channels), F32),
-            pltpu.VMEM((128, BLOCK), F32),
-        ],
+        in_specs=ins,
+        out_specs=outs,
+        out_shape=backward_outs(seqs, length, channels, n2, small),
+        scratch_shapes=backward_scratch(channels, n2),
         compiler_params=pltpu.CompilerParams(vmem_limit_bytes=56 * 2**20),
         name="ssd_backward",
     )(dy, x, cx, bc, cbc, dt, cols, segrow, states, *shared)
@@ -413,13 +437,14 @@
     return t, t + 1 - 2 * (t % 2), (t + 2) % 4
 
 
-def greet(n):
+def greet(n, more=()):
     place, at = ring_place(n)
     _, other, across = tensor_place()
     sem = pltpu.get_barrier_semaphore()
-    for target in ({"dp": at(place + 1)}, {"dp": at(place - 1)}, {"tensor": other}, {"tensor": across}):
+    targets = [{"dp": at(place + 1)}, {"dp": at(place - 1)}, {"tensor": other}, {"tensor": across}, *more]
+    for target in targets:
         pl.semaphore_signal(sem, inc=1, device_id=target, device_id_type=MESH)
-    pl.semaphore_wait(sem, 4)
+    pl.semaphore_wait(sem, len(targets))
 
 
 def remote(src, dst, send_sem, recv_sem, target):
@@ -683,45 +708,54 @@
         self.me, self.other, self.across = tensor_place()
 
     def copy(self, kind, part):
+        src, dst = ((0, 1), (1, 2), (0, 3))[kind]
         return remote(
-            self.hold.at[kind, 0, part],
-            self.hold.at[kind, 1, part],
+            self.hold.at[src, part],
+            self.hold.at[dst, part],
             self.send_sem.at[kind, part],
             self.recv_sem.at[kind, part],
             {"tensor": self.across if kind == 1 else self.other},
         )
 
-    def step(self, j, store):
-        stage, part = j // self.parts, j % self.parts
+    def step(self, j, store, wait=True):
+        late = j // (2 * self.parts)
+        near = j - 2 * self.parts
+        stage = (1 - late) * (j % 2) + late * (2 + near // self.parts)
+        part = (1 - late) * (j // 2) + late * (near % self.parts)
         x, core = self.me // 2, self.me % 2
         value = self.term(2 * ((x + 1 - stage // 2) % 2) + (core + 1 - stage % 2) % 2, part)
 
         @pl.when(stage == 0)
         def _():
-            self.hold[0, 0, part] = value.astype(BF16)
+            self.hold[0, part] = value.astype(BF16)
             self.copy(0, part).start()
 
         @pl.when(stage == 1)
         def _():
             self.copy(0, part).wait_recv()
-            self.hold[1, 0, part] = (value + self.hold[0, 1, part].astype(F32)).astype(BF16)
+            self.hold[1, part] = (value + self.hold[1, part].astype(F32)).astype(BF16)
             self.copy(1, part).start()
 
         @pl.when(stage == 2)
         def _():
-            self.hold[2, 0, part] = value.astype(BF16)
+            self.copy(0, part).wait_send()
+            self.hold[0, part] = value.astype(BF16)
             self.copy(2, part).start()
 
         @pl.when(stage == 3)
         def _():
-            self.copy(2, part).wait_recv()
-            store(part, value + self.hold[2, 1, part].astype(F32))
-
-    def finish(self, store):
+            store(part, value + self.arrived(part) if wait else value)
+
+        return value, 2 * ((x + 1 - stage // 2) % 2) + (core + 1 - stage % 2) % 2, part
+
+    def arrived(self, part):
+        self.copy(2, part).wait_recv()
+        self.copy(1, part).wait_recv()
+        return self.hold[3, part].astype(F32) + self.hold[2, part].astype(F32)
+
+    def finish(self):
         for part in range(self.parts):
-            self.copy(1, part).wait_recv()
-            store(part, self.hold[1, 1, part].astype(F32))
-            for kind in range(3):
+            for kind in (1, 2):
                 self.copy(kind, part).wait_send()
 
 
@@ -733,92 +767,178 @@
     return term
 
 
-def out_kernel(
-    n, normed_ref, g_ref, u_ref, dz_ref, wo_ref, mixed_ref, gout_ref, gz_ref, out_slots, z_slots, hold, *sems
-):
-    seqs, length = mixed_ref.shape[0], normed_ref.shape[0] // mixed_ref.shape[0]
-    piece = mixed_ref.shape[1]
+def back_kernel(n, *refs):
+    (normed_ref, g_ref, u_ref, dz_ref, wo_ref, hidden_ref), refs = refs[:6], refs[6:]
+    ins, refs = refs[:15], refs[15:]
+    (out_ref, gout_ref, gz_ref), refs = refs[:3], refs[3:]
+    outs, refs = refs[:5], refs[5:]
+    scratch, refs = refs[:7], refs[7:]
+    normed, dz, wo, g_cols, u_cols, out_slots, z_slots, hold, load_sem, stream_sem = refs[:10]
+    sems = refs[10:]
+
+    k = pl.program_id(0)
+    blocks = 4
+    piece = out_ref.shape[1]
+    length = blocks * BLOCK
     count = g_ref.shape[1] // n
     half = gz_ref.shape[1] // 2
-    greet(n)
+    place, at = ring_place(n)
+
+    loads = [
+        pltpu.make_async_copy(src, dst, load_sem.at[i])
+        for i, (src, dst) in enumerate(((normed_ref, normed), (dz_ref, dz), (wo_ref, wo)))
+    ]
+
+    def streams(k):
+        copies = []
+        for way in (0, 1):
+            d = at(place - (1 - 2 * way) * (1 + k))
+            for i, (src, dst) in enumerate(((g_ref, g_cols), (u_ref, u_cols))):
+                copies.append(
+                    pltpu.make_async_copy(
+                        src.at[:, span(d * count, count, 128)], dst.at[way], stream_sem.at[i, way]
+                    )
+                )
+        return copies
+
+    @pl.when(k == 0)
+    def _():
+        for copy in loads + streams(0):
+            copy.start()
+        greet(n)
+        for copy in loads:
+            copy.wait()
+
+    for copy in streams(k):
+        copy.wait()
+
+    def half_product(a_ref, b_ref):
+        def term(way, d):
+            return dot_tn(a_ref[way], b_ref[:, pl.ds(way * half, half)])
+
+        return term
+
+    out_ring = RingScatter(n, half_product(g_cols, normed), out_slots, sems[0:2])
+    z_ring = RingScatter(n, half_product(u_cols, dz), z_slots, sems[2:4])
+    for way in (0, 1):
+        value = out_ring.step(way, k)
+
+        @pl.when(k == n - 1)
+        def _():
+            gout_ref[pl.ds(way * half, half), :] = out_ring.last(way, value).T
+
+    for way in (0, 1):
+        value = z_ring.step(way, k)
+
+        @pl.when(k == n - 1)
+        def _():
+            gz_ref[:, pl.ds(way * half, half)] = z_ring.last(way, value)
+
+    @pl.when(k < n - 1)
+    def _():
+        for copy in streams(k + 1):
+            copy.start()
 
     def mixed_term(t, part):
-        return dot(normed_ref[span(part * length + t * piece, piece, 16), :], wo_ref[...])
-
-    rows = RowScatter(seqs, mixed_term, hold, sems[0:2])
-    rings = [
-        RingScatter(n, product_term(g_ref, normed_ref, count), out_slots, sems[2:4]),
-        RingScatter(n, product_term(u_ref, dz_ref, count), z_slots, sems[4:6]),
-    ]
+        return dot(normed[span(part * length + t * piece, piece, 16), :], wo[...])
 
     def store(part, value):
-        mixed_ref[part] = value
-
-    def out_step(k, _):
-        for way in (0, 1):
-            value = rings[0].step(way, k)
-
-            @pl.when(k == n - 1)
-            def _():
-                gout_ref[pl.ds(way * half, half), :] = rings[0].last(way, value).T
-
-        rows.step(k, store)
-        return 0
-
-    def z_step(k, _):
-        for way in (0, 1):
-            value = rings[1].step(way, k)
-
-            @pl.when(k == n - 1)
-            def _():
-                gz_ref[:, pl.ds(way * half, half)] = rings[1].last(way, value)
-
-        return 0
-
-    lax.fori_loop(0, n, out_step, 0)
-    lax.fori_loop(0, n, z_step, 0)
-
-    def add(part, value):
-        mixed_ref[part] += value
-
-    rows.finish(add)
-    for ring in rings:
-        ring.finish()
-
-
-def scatter_out(n, piece, normed, g, u, dz, w_out):
-    tokens, width = normed.shape
-    model = g.shape[1]
-    seqs = tokens // (4 * piece)
+        out_ref[0] = (hidden_ref[0].astype(F32) + value).astype(BF16)
+
+    rows = RowScatter(2, mixed_term, hold, sems[4:6])
+    rows.step(k, store)
+
+    backward_block(k // blocks, k % blocks, *ins, *outs, *scratch)
+
+    @pl.when(k == n - 1)
+    def _():
+        rows.finish()
+        out_ring.finish()
+        z_ring.finish()
+
+
+def backward_all(n, small, hidden, normed, g, u, dz, w_out, dy, x, cx, bc, cbc, dt, cols, segrow, states, shared):
+    seqs, length, channels = x.shape
+    n2, heads = bc.shape[2], dt.shape[2]
+    tokens, model = g.shape
+    piece = hidden.shape[1]
     count = model // n
+    blocks = length // BLOCK
     sem = pltpu.SemaphoreType.DMA
-    vmem = pl.BlockSpec(memory_space=pltpu.VMEM)
+    anywhere = pl.BlockSpec(memory_space=pl.ANY)
+    ins, outs = backward_specs(channels, n2, heads, small, lambda k: (k // blocks, blocks - 1 - k % blocks))
+    late = lambda k: (jnp.maximum(k - (n - 2), 0), 0, 0)
+    part = pl.BlockSpec((1, piece, model), late)
+    single = pl.BlockSpec((1, piece, model), late, pipeline_mode=pl.Buffered(1))
+    whole = lambda *shape: pl.BlockSpec(shape, lambda k: (0,) * len(shape))
     return pl.pallas_call(
-        functools.partial(out_kernel, n),
-        in_specs=[vmem] * 5,
-        out_specs=[vmem] * 3,
+        functools.partial(back_kernel, n),
+        grid=(n,),
+        in_specs=[anywhere] * 5 + [single] + ins,
+        out_specs=[part, whole(channels, count), whole(count, channels)] + outs,
         out_shape=[
-            jax.ShapeDtypeStruct((seqs, piece, model), F32),
-            jax.ShapeDtypeStruct((width, count), F32),
-            jax.ShapeDtypeStruct((count, width), F32),
-        ],
-        scratch_shapes=[
-            pltpu.VMEM((2, n, count, width // 2), BF16),
-            pltpu.VMEM((2, n, count, width // 2), BF16),
-            pltpu.VMEM((3, 2, seqs, piece, model), BF16),
+            jax.ShapeDtypeStruct(hidden.shape, BF16),
+            jax.ShapeDtypeStruct((channels, count), F32),
+            jax.ShapeDtypeStruct((count, channels), F32),
         ]
-        + [sem((3, seqs))] * 2 + [sem((2, n - 1))] * 4,
+        + backward_outs(seqs, length, channels, n2, small),
+        scratch_shapes=backward_scratch(channels, n2)
+        + [
+            pltpu.VMEM((tokens, channels), BF16),
+            pltpu.VMEM((tokens, channels), BF16),
+            pltpu.VMEM((channels, model), BF16),
+            pltpu.VMEM((2, tokens, count), BF16),
+            pltpu.VMEM((2, tokens, count), BF16),
+            pltpu.VMEM((2, n, count, channels // 2), BF16),
+            pltpu.VMEM((2, n, count, channels // 2), BF16),
+            pltpu.VMEM((4, seqs, piece, model), BF16),
+            sem((3,)),
+            sem((2, 2)),
+        ]
+        + [sem((2, n - 1))] * 4
+        + [sem((3, seqs))] * 2,
         compiler_params=pltpu.CompilerParams(
-            collective_id=1, has_side_effects=True, vmem_limit_bytes=60 * 2**20
+            collective_id=1, has_side_effects=True, vmem_limit_bytes=63 * 2**20
         ),
-        name="scatter_out",
-    )(normed, g, u, dz, w_out)
+        name="backward_all",
+    )(normed, g, u, dz, w_out, hidden, dy, x, cx, bc, cbc, dt, cols, segrow, states, *shared)
+
+
+class Fold:
+    def __init__(self, n, total, came, sems):
+        self.total, self.came = total, came
+        self.send_sem, self.recv_sem = sems
+        dp = lax.axis_index("dp")
+        _, other, across = tensor_place()
+        partners, ahead = [], 1
+        while ahead < n:
+            partners.append({"dp": dp + ahead * (1 - 2 * ((dp // ahead) % 2))})
+            ahead *= 2
+        self.over_dp = partners
+        self.partners = partners + [{"tensor": other}, {"tensor": across}]
+
+    def copy(self, r):
+        return remote(
+            self.total.at[r], self.came.at[r], self.send_sem.at[r], self.recv_sem.at[r], self.partners[r]
+        )
+
+    def start(self, r):
+        self.copy(r).start()
+
+    def take(self, r):
+        self.copy(r).wait_recv()
+        self.total[r + 1] = self.total[r] + self.came[r]
+
+    def finish(self):
+        for r in range(len(self.partners)):
+            self.copy(r).wait_send()
 
 
 def in_kernel(
-    n, u_ref, dz_ref, dx_ref, wz_ref, wx_ref, wb_ref, dbc_ref,
-    din_ref, gx_ref, gb_ref,
-    x_slots, b_slots, hold, bc_hold, low, pair_hold, swap, *sems,
+    n, u_hbm, dz_hbm, dx_hbm, wz_hbm, wx_hbm, wb_hbm, dbc_hbm, gx_in, gbc_in, gh_in, gate_in, gain_ref,
+    din_ref, gx_ref, gb_ref, sums_ref,
+    u_ref, dz_ref, dx_ref, wz_ref, wx_ref, wb_ref, dbc_ref,
+    x_slots, b_slots, hold, bc_hold, low, swap, pre, total, came, load_sem, *sems,
 ):
     seqs, piece = din_ref.shape[:2]
     tokens, model = u_ref.shape
@@ -827,7 +947,11 @@
     half = gx_ref.shape[1] // 2
     me, other, across = tensor_place()
     core = me % 2
-    greet(n)
+
+    moves = ((dx_hbm, dx_ref), (u_hbm, u_ref), (dbc_hbm, dbc_ref), (dz_hbm, dz_ref), (wz_hbm, wz_ref), (wx_hbm, wx_ref), (wb_hbm, wb_ref))
+    loads = [pltpu.make_async_copy(src, dst, load_sem.at[i]) for i, (src, dst) in enumerate(moves)]
+    for load in loads[:3]:
+        load.start()
 
     def bc_term(t, part):
         return dbc_ref[span(part * length + t * piece, piece, 16), :].astype(F32)
@@ -837,33 +961,56 @@
         return dot_nt(dz_ref[at, :], wz_ref[...]) + dot_nt(dx_ref[at, :], wx_ref[...])
 
     def b_term(way, d):
-        cols = u_ref.shape[1] // n // 4
-        total = 0.0
+        total_rows = 0.0
         for t, which in ((me, 0), (other, 1)):
             for part in range(seqs):
-                a = u_ref[span(part * length + t * piece, piece, 16), span(d * count + core * count // 2, count // 2, 128)]
-                total = total + dot_tn(a, low[which, part])
-        return total[way * cols : (way + 1) * cols]
+                rows = span(part * length + t * piece, piece, 16)
+                cols = span(d * count + core * count // 2, count // 2, 128)
+                total_rows = total_rows + dot_tn(u_ref[rows, cols], low[which, part])
+        return total_rows[way * count // 4 : (way + 1) * count // 4]
 
     bc_rows = RowScatter(seqs, bc_term, bc_hold, sems[0:2])
     in_rows = RowScatter(seqs, in_term, hold, sems[2:4])
     x_ring = RingScatter(n, product_term(u_ref, dx_ref, count), x_slots, sems[4:6])
     b_ring = RingScatter(n, b_term, b_slots, sems[6:8])
     pair_send, pair_recv, swap_send, swap_recv = sems[8:12]
+    fold = Fold(n, total, came, sems[12:14])
+    rounds = len(fold.partners)
+    pair = remote(low.at[0], low.at[1], pair_send, pair_recv, {"tensor": other})
+
+    total[0] = jnp.zeros_like(total[0])
+    total[0, 0:6, :] = gx_in[0:6, :]
+    total[0, 6:7, :] = gate_in[...]
+    total[0, 7:8, 0:128] = gh_in[0:1, :]
+    total[0, 7:8, 128:256] = gh_in[1:2, :]
+    total[0, 8:13, 0 : gbc_in.shape[1]] = gbc_in[0:5, :]
+    pre[...] = jnp.zeros_like(pre)
+    greet(n, fold.over_dp)
+    for load in loads[:3]:
+        load.wait()
+    for load in loads[3:]:
+        load.start()
 
     def bc_store(part, value):
-        pair_hold[part] = value
-
-    def bc_step(j, _):
-        bc_rows.step(j, bc_store)
-        return 0
-
-    lax.fori_loop(0, 4 * seqs, bc_step, 0)
+        low[0, part] = value.astype(BF16)
 
     def store(part, value):
+        value = value + dot_nt(low[0, part], wb_ref[...])
         din_ref[part] = value
-
-    def step(k, _):
+        pre[...] += jnp.sum(
+            value * u_ref[span(part * length + me * piece, piece, 16), :].astype(F32), axis=0, keepdims=True
+        )
+
+    def row_step(j):
+        value, t, part = in_rows.step(j, store, wait=False)
+
+        @pl.when(j < 3 * seqs)
+        def _():
+            pre[...] += jnp.sum(
+                value * u_ref[span(part * length + t * piece, piece, 16), :].astype(F32), axis=0, keepdims=True
+            )
+
+    def ring_step(k):
         for way in (0, 1):
             value = x_ring.step(way, k)
 
@@ -871,20 +1018,7 @@
             def _():
                 gx_ref[:, pl.ds(way * half, half)] = x_ring.last(way, value)
 
-        in_rows.step(k, store)
-        return 0
-
-    lax.fori_loop(0, n, step, 0)
-
-    def bc_add(part, value):
-        low[0, part] = (pair_hold[part] + value).astype(BF16)
-
-    bc_rows.finish(bc_add)
-    pair = remote(low.at[0], low.at[1], pair_send, pair_recv, {"tensor": other})
-    pair.start()
-    pair.wait_recv()
-
-    def b_step(k, _):
+    def b_step(k):
         for way in (0, 1):
             value = b_ring.step(way, k)
 
@@ -892,62 +1026,108 @@
             def _():
                 swap[0, pl.ds(way * count // 4, count // 4), :] = b_ring.last(way, value)
 
+    ring_step(0)
+    for load in loads[3:]:
+        load.wait()
+    for j in range(2 * seqs):
+        bc_rows.step(j, bc_store)
+    row_step(0)
+
+    def step(k, _):
+        row_step(k)
+        ring_step(k)
+
+        @pl.when(k == 1)
+        def _():
+            for j in range(2 * seqs, 4 * seqs):
+                bc_rows.step(j, bc_store)
+            pair.start()
+            pair.wait_recv()
+
+        @pl.when(k >= 2)
+        def _():
+            b_step(k - 2)
+
         return 0
 
-    lax.fori_loop(0, n, b_step, 0)
+    lax.fori_loop(1, n, step, 0)
+    gain = gain_ref[...]
+    width = total.shape[2]
+    for i in range(model // width):
+        at = slice(i * width, (i + 1) * width)
+        total[0, 13 + i : 14 + i, :] = pre[:, at] / gain[:, at]
+    fold.start(0)
+    b_step(n - 2)
+    fold.take(0)
+    fold.start(1)
+    b_step(n - 1)
     cross = remote(swap.at[0], swap.at[1], swap_send.at[0], swap_recv.at[0], {"tensor": across})
     cross.start()
-
-    def add(part, value):
-        din_ref[part] += value + dot_nt(low[0, part], wb_ref[...])
-
-    in_rows.finish(add)
+    fold.take(1)
+    fold.start(2)
     cross.wait_recv()
     swap[2] = swap[0] + swap[1]
-    fold = remote(swap.at[2], swap.at[3], swap_send.at[1], swap_recv.at[1], {"tensor": other})
-    fold.start()
+    back = remote(swap.at[2], swap.at[3], swap_send.at[1], swap_recv.at[1], {"tensor": other})
+    back.start()
+    fold.take(2)
+    fold.start(3)
     gb_ref[span(core * count // 2, count // 2, 16), :] = swap[2]
-    fold.wait_recv()
+    din_ref[0] += in_rows.arrived(0)
+    fold.take(3)
+    fold.start(4)
+    for part in range(1, seqs):
+        din_ref[part] += in_rows.arrived(part)
+    back.wait_recv()
     gb_ref[span((1 - core) * count // 2, count // 2, 16), :] = swap[3]
-    pair.wait_send()
-    cross.wait_send()
-    fold.wait_send()
-    for ring in (x_ring, b_ring):
-        ring.finish()
-
-
-def scatter_in(n, piece, u, dz, dx, w_z, w_x, w_bc, dbc):
+    fold.take(4)
+    sums_ref[0:8, :] = total[rounds - 2, 0:8, :]
+    sums_ref[8:16, :] = total[rounds, 8:16, :]
+    for copy in (pair, cross, back):
+        copy.wait_send()
+    for part in (bc_rows, in_rows, x_ring, b_ring, fold):
+        part.finish()
+
+
+def scatter_in(n, piece, u, dz, dx, w_z, w_x, w_bc, dbc, gx, gbc, gh, grad_gate, gain):
     tokens, model = u.shape
     width = dz.shape[1]
     small = dbc.shape[1]
     seqs = tokens // (4 * piece)
     count = model // n
+    rounds = 5
     sem = pltpu.SemaphoreType.DMA
     vmem = pl.BlockSpec(memory_space=pltpu.VMEM)
+    anywhere = pl.BlockSpec(memory_space=pl.ANY)
+    big = (u, dz, dx, w_z, w_x, w_bc, dbc)
     return pl.pallas_call(
         functools.partial(in_kernel, n),
-        in_specs=[vmem] * 7,
-        out_specs=[vmem] * 3,
+        in_specs=[anywhere] * 7 + [vmem] * 5,
+        out_specs=[vmem] * 4,
         out_shape=[
             jax.ShapeDtypeStruct((seqs, piece, model), F32),
             jax.ShapeDtypeStruct((count, width), F32),
             jax.ShapeDtypeStruct((count, small), F32),
+            jax.ShapeDtypeStruct((16, width), F32),
         ],
-        scratch_shapes=[
+        scratch_shapes=[pltpu.VMEM(a.shape, BF16) for a in big]
+        + [
             pltpu.VMEM((2, n, count, width // 2), BF16),
             pltpu.VMEM((2, n, count // 4, small), BF16),
-            pltpu.VMEM((3, 2, seqs, piece, model), BF16),
-            pltpu.VMEM((3, 2, seqs, piece, small), BF16),
+            pltpu.VMEM((4, seqs, piece, model), BF16),
+            pltpu.VMEM((4, seqs, piece, small), BF16),
             pltpu.VMEM((2, seqs, piece, small), BF16),
-            pltpu.VMEM((seqs, piece, small), F32),
             pltpu.VMEM((4, count // 2, small), F32),
+            pltpu.VMEM((1, model), F32),
+            pltpu.VMEM((rounds + 1, 16, width), F32),
+            pltpu.VMEM((rounds, 16, width), F32),
+            sem((len(big),)),
         ]
-        + [sem((3, seqs))] * 4 + [sem((2, n - 1))] * 4 + [sem(())] * 2 + [sem((2,))] * 2,
+        + [sem((3, seqs))] * 4 + [sem((2, n - 1))] * 4 + [sem(())] * 2 + [sem((2,))] * 2 + [sem((rounds,))] * 2,
         compiler_params=pltpu.CompilerParams(
-            collective_id=2, has_side_effects=True, vmem_limit_bytes=62 * 2**20
+            collective_id=2, has_side_effects=True, vmem_limit_bytes=63 * 2**20
         ),
         name="scatter_in",
-    )(u, dz, dx, w_z, w_x, w_bc, dbc)
+    )(*big, gx, gbc, gh, grad_gate, gain)
 
 
 def rms_scale(values):
@@ -1017,7 +1197,7 @@
     n2 = conv_bc.shape[1]
     columns = w_bcdt.shape[1]
     tensor = lax.axis_index("tensor")
-    kernels = n_dp == 8 and n_tensor == 4
+    kernels = n_dp == 8 and n_tensor == 4 and seqs == 2 and length == 4 * BLOCK
 
     x_piece = hidden.astype(F32)
     scale_in = rms_scale(x_piece)
@@ -1056,41 +1236,44 @@
     dy = (d_gated * silu_z).astype(BF16)
     dz = (d_gated * y_flat * (sig_z * (1.0 + z * (1.0 - sig_z)))).astype(BF16)
 
-    scatter = functools.partial(scatter_out, n_dp) if kernels else scatter_out_plain
-    mixed, grad_out, grad_z = scatter(piece, normed, g, u, dz, w_o)
-    out_hidden = (x_piece + mixed).astype(BF16)
-
-    dx, d_bc, d_dt, gx, gbc, gh = ssd_backward(
-        dy.reshape(seqs, length, channels), x, cx, bc, cbc, dt, cols, segrow, states, shared
-    )
-    d_dt = lax.dynamic_update_slice_in_dim(
-        jnp.zeros((seqs, length, w_bc.shape[1] - n2), F32), d_dt, tensor * heads, 2
-    )
-    dbc = jnp.concatenate([d_bc, d_dt], axis=2).astype(BF16).reshape(tokens, -1)
-
-    scatter = functools.partial(scatter_in, n_dp) if kernels else scatter_in_plain
-    d_in, grad_x, grad_bc = scatter(piece, u, dz, dx.reshape(tokens, channels), w_z, w_x, w_bc, dbc)
-
-    grad_pre = jnp.sum(d_in * x_piece * scale_in, axis=(0, 1))
+    x, bc = x.astype(BF16), bc.astype(BF16)
+    back_args = (dy.reshape(seqs, length, channels), x, cx, bc, cbc, dt, cols, segrow, states, shared)
+    if kernels:
+        out_hidden, grad_out, grad_z, *rest = backward_all(n_dp, w_bc.shape[1], hidden, normed, g, u, dz, w_o, *back_args)
+    else:
+        mixed, grad_out, grad_z = scatter_out_plain(piece, normed, g, u, dz, w_o)
+        out_hidden = (x_piece + mixed).astype(BF16)
+        rest = ssd_backward(w_bc.shape[1], *back_args)
+    dx, dbc, gx, gbc, gh = rest
+    in_args = (piece, u, dz, dx.reshape(tokens, channels), w_z, w_x, w_bc, dbc.reshape(tokens, -1))
+    if kernels:
+        d_in, grad_x, grad_bc, sums = scatter_in(n_dp, *in_args, gx, gbc, gh, grad_gate[None], pre_gain[None])
+        grad_pre = sums[13:].reshape(-1)[:model]
+        grad_conv_bc = sums[8:13, :n2]
+    else:
+        d_in, grad_x, grad_bc = scatter_in_plain(*in_args)
+        grad_pre = jnp.sum(d_in * x_piece * scale_in, axis=(0, 1))
+        steps = jnp.pad(gh[:2], ((0, 0), (0, channels - gh.shape[1])))
+        sums = lax.psum(jnp.concatenate([gx[:6], grad_gate[None], steps]), "dp")
+        sums = jnp.concatenate([sums[:7], jnp.concatenate([sums[7, :128], sums[8, : channels - 128]])[None]])
+        grad_conv_bc, grad_pre = lax.psum((gbc[:5], grad_pre), ("dp", "tensor"))
+
     gain_grad = d_in * pre_gain
     d_hidden = cotangent.astype(F32) + scale_in * gain_grad - x_piece * scale_in**3 * jnp.mean(
         gain_grad * x_piece, axis=-1, keepdims=True
     )
-    grad_skip = gx[5].reshape(heads, -1).sum(axis=1)
-    small_dp = lax.psum((gx[:5], gh[0, :heads], gh[1, :heads], grad_skip, grad_gate), "dp")
-    small_all = lax.psum((gbc[:5], grad_pre), ("dp", "tensor"))
     return (
         out_hidden,
         d_hidden,
-        small_all[1],
+        grad_pre,
         jnp.stack([grad_z, grad_x]),
         grad_bc[:, :columns],
-        small_dp[0],
-        small_all[0],
-        small_dp[1],
-        small_dp[2],
-        small_dp[3],
-        small_dp[4],
+        sums[:5],
+        grad_conv_bc,
+        sums[7, :heads],
+        sums[7, 128 : 128 + heads],
+        sums[5].reshape(heads, -1).sum(axis=1),
+        sums[6],
         grad_out,
     )
 

time: 668 us -> 515 us (0.77)
  blocking collectives: 88.9 us -> 10.4 us
  Pallas kernels: 445 us -> 376 us
    psum x2 -> x0, blocking collectives: 78.3 us -> none  [the longest x1 41.8 us: local(): small_all = lax.psum((gbc[:5], grad_pre), ('dp', 'tensor'))]
    pallas_call x3 -> x2, Pallas kernels: 283 us -> 214 us  [the longest x1 129 us: backward_all(): pl.pallas_call(functools.partial(back_kernel, n), grid=(n,), in_specs=[an...]
where the time goes in v2:
time: 515 us; the launch traced here: 507 us
  Pallas kernels  376 us (73%)
  matrix products  56.2 us (11%)
  other arithmetic  33.2 us (6%)
  local copies, waits for them, and re-layouts  29.9 us (6%)
  blocking collectives  10.4 us (2%)
    pallas_call x1, Pallas kernels, gather_all(): pl.pallas_call(functools.partial(gather_kernel, n), in_specs=[anywhere] *...  136 us
    pallas_call x1, Pallas kernels, backward_all(): pl.pallas_call(functools.partial(back_kernel, n), grid=(n,), in_specs=[an...  129 us
    pallas_call x1, Pallas kernels, scatter_in(): pl.pallas_call(functools.partial(in_kernel, n), in_specs=[anywhere] * 7 +...  85.2 us
    dot_general x3, matrix products, dot(): return jnp.dot(a, b, preferred_element_type=F32)  45 us
    pallas_call x1, Pallas kernels, ssd_forward(): pl.pallas_call(forward_kernel, grid=(seqs, blocks), in_specs=[tok(channel...  25.5 us
    convert_element_type x1, other arithmetic, local(): dy = (d_gated * silu_z).astype(BF16)  16 us
    another operation x8, local copies, waits for them, and re-layouts, column_masks(): return jnp.stack(stacked, axis=-1)  13.8 us
    dot_general x1, matrix products, dot_nt(): lax.dot_general(a, b, (((1,), (1,)), ((), ())), preferred_element_type=F32)  11.2 us

profile of v2, /device:TPU:0, one launch (start us, length us, event | category | flops | bytes accessed | tf_op | source)
XLA Modules:
  0.0 507.0 jit_solution(18048362552241577782)
XLA Ops:
  0.6 2.1 fusion.3
  2.7 0.7 broadcast_in_dim.28
  3.5 0.1 broadcast_in_dim_reshape.3.skip_ref.refs_19_
  3.5 0.7 reshape.98
  4.3 0.1 slice.73
  4.3 0.1 copy.73
  4.4 0.1 broadcast_bitcast_fusion
  4.5 0.9 fusion.21
  5.4 0.1 copy.72
  5.6 0.9 fusion.17
  6.6 1.1 copy.59
  7.7 1.4 copy.68
  9.0 1.3 copy.66
  10.4 1.3 copy.67
  11.7 1.3 copy.65
  13.1 1.3 copy.64
  14.4 1.4 copy.69
  15.8 1.0 stack.68
  16.8 4.7 stack.69.cols_ref.refs_12_
  21.6 0.5 fusion.5.u_ref
  22.2 1.4 copy-done.2
  23.5 0.3 copy-done.10
  23.8 0.1 copy-done.11
  23.9 135.9 %gather_all.1 = (bf16[2,1024,2048]{2,1,0:T(8,128)(2,1)}, bf16[2,1024,2048]{2,1,0:T(8,128)(2,1)}, bf16[2048,1024]{1,0:T(8,128)(2,1)S(1)}, bf16[2048,1024]{1,0:T(8...) custom-call(bf16[2,256,2048]{2,1,0:T(8,128)(2,1)S(1)} %fusion.5.u_ref, ...), custom_call_target="tpu_custom_call" | custom-call | tf_op jit(solution)/shard_map/gather_all/pallas_call | solution.py:637
  159.9 10.6 %fusion.11 = f32[2,1024,384]{2,1,0:T(8,128)S(1)} fusion(bf16[2,1024,2048]{2,1,0:T(8,128)(2,1)} %get-tuple-element.34, bf16[2048,384]{1,0:T(8,128)(2,1)S(1)} %get-tuple-element.36.wb_hbm), kind=kOutput, calls=%fused_computation.25 | convolution fusion | flops 3221225472 | bytes 13107200 | tf_op jit(solution)/shard_map/dot_general | solution.py:34
  170.6 0.3 constant_dynamic-slice_fusion.dt_ref.refs_11_
  170.9 1.2 slice.97.refs_9_
  172.1 1.5 slice.71.bc_ref
  173.6 11.2 %fusion.23 = f32[2048,1024]{1,0:T(8,128)} fusion(bf16[2048,2048]{1,0:T(8,128)(2,1)S(1)} %bitcast.90, bf16[1024,2048]{1,0:T(8,128)(2,1)S(1)} %get-tuple-element.40.refs_4_), kind=kOutput, calls=%fused_computation.62 | convolution fusion | flops 8589934592 | bytes 20971520 | tf_op jit(solution)/shard_map/dot_general | solution.py:38
  184.8 14.2 %fusion.22 = (bf16[2,1024,1024]{2,1,0:T(8,128)(2,1)}, f32[2,1024,1024]{2,1,0:T(8,128)}) fusion(bf16[2,1024,2048]{2,1,0:T(8,128)(2,1)} %get-tuple-element.34, bf16[2048,1024]{1,0:T(8,128)(2,1)S(1)} %get-tuple-element.35.wx_hbm), kind=kOutput, calls=%fused_computation.61 | convolution fusion | flops 8592031744 | bytes 25165824 | tf_op jit(solution)/shard_map/dot_general | solution.py:34
  199.0 25.5 %ssd_forward.1 = (f32[2,1024,1024]{2,1,0:T(8,128)}, f32[2,1024,1024]{2,1,0:T(8,128)}, f32[2,1024,256]{2,1,0:T(8,128)S(1)}, bf16[2,4,128,1024]{3,2,1,0:T(8,128)(2,1)}) custom-call(f32[2,1024,1024]{2,1,0:T(8,128)} %get-tuple-element.128.x_ref, f32[2,1024,256]{2,1,0:T(8,128)} %slice.71.bc_ref, f32[2,1024,16]{2,1,0:T(8,128)S(1)} %constant_dynamic-slice_fusion.dt_ref.refs_11_, ...), custom_call_target="tpu_custom_call" | custom-call | tf_op jit(solution)/shard_map/ssd_forward/pallas_call | solution.py:339
  224.5 20.2 %multiply_reduce_fusion.2 = (f32[2048]{0:T(1024)S(1)}, f32[2048]{0:T(1024)S(1)}, f32[2048,1024]{1,0:T(8,128)}) fusion(f32[2,1024,1024]{2,1,0:T(8,128)} %get-tuple-element.37, f32[2048,1024]{1,0:T(8,128)} %fusion.23, f32[1024]{0:T(1024)S(1)} %copy-done.26, bf16[2048,2048]{1,0:T(8,128)(2,1)} %bitcast.83, bf16[2048,1024]{1,0:T(8,128)(2,1)S(1)} %copy-done.7), kind=kOutput, calls=%fused_computation.9 | convolution fusion | flops 8610902016 | bytes 37769216 | tf_op jit(solution)/shard_map/dot_general | solution.py:34
  244.8 10.4 %psum.7 = f32[2,2048]{1,0:T(2,128)S(1)} all-reduce(f32[2,2048]{1,0:T(2,128)S(1)} %pad_maximum_fusion.1), channel_id=1, replica_groups=mesh['dp'=8,'tensor'=4] {'tensor'}, use_global_device_ids=true, to_apply=%region_3.4 | all-reduce | flops 4096 | bytes 32768 | tf_op jit(solution)/shard_map/psum | solution.py:1231
  255.2 16.0 %multiply_convert_fusion = (bf16[2048,1024]{1,0:T(8,128)(2,1)}, bf16[2048,1024]{1,0:T(8,128)(2,1)}, f32[1024]{0:T(1024)}, bf16[2048,1024]{1,0:T(8,128)(2,1)}) fusion(f32[2048,1024]{1,0:T(8,128)} %get-tuple-element.126, f32[2048]{0:T(1024)S(1)} %bitcast.101, f32[2048,1024]{1,0:T(8,128)} %fusion.23, f32[2048]{0:T(1024)S(1)} %multiply_multiply_fusion, ...), kind=kLoop, calls=%fused_computation.5 | loop fusion | flops 52427776 | bytes 37781504 | tf_op jit(solution)/shard_map/convert_element_type | solution.py:1236
  271.2 129.3 %backward_all.1 = (bf16[2,256,2048]{2,1,0:T(8,128)(2,1)}, f32[1024,256]{1,0:T(8,128)}, f32[256,1024]{1,0:T(8,128)}, bf16[2,1024,1024]{2,1,0:T(8,128)(2,1)}, bf16...) custom-call(bf16[2048,1024]{1,0:T(8,128)(2,1)} %get-tuple-element.109.refs_0_, ...), custom_call_target="tpu_custom_call" | custom-call | tf_op jit(solution)/shard_map/backward_all/pallas_call | solution.py:874
  400.5 85.2 %scatter_in.1 = (f32[2,256,2048]{2,1,0:T(8,128)}, f32[256,1024]{1,0:T(8,128)}, f32[256,384]{1,0:T(8,128)}, f32[16,1024]{1,0:T(8,128)}) custom-call(bf16[2048,2048]{1,0:T(8,128)(2,1)} %bitcast.85, bf16[2048,1024]{1,0:T(8,128)(2,1)} %get-tuple-element.107.refs_3_.dz_hbm, bf16[2048,1024]{1,0:T(8,128)(2,1)} %bitcast.91, bf16[2048,1024]{1,0:T(8,128)(2,1)} %copy-done.6, ...), custom_call_target="tpu_custom_call" | custom-call | tf_op jit(solution)/shard_map/scatter_in/pallas_call | solution.py:1102
  485.7 3.2 pad_maximum_fusion
  488.9 0.9 copy.70
  489.8 0.5 slice_bitcast_fusion.1
  490.3 3.5 fusion.8
  493.9 5.4 %fusion.7 = f32[2,256,2048]{2,1,0:T(8,128)} fusion(bf16[2,256,2048]{2,1,0:T(8,128)(2,1)S(1)} %copy-done.20, bf16[2,256,2048]{2,1,0:T(8,128)(2,1)S(1)} %copy-done.3, f32[2,256,2048]{2,1,0:T(8,128)} %get-tuple-element.50, f32[2,256]{1,0:T(2,128)S(1)} %broadcast_multiply_fusion.1, f32[2,256]{1,0:T(2,128)S(1)} %get-tuple-element.124, f32[2048]{0:T(1024)S(1)} %copy-done.24, ...), kind=kLoop, calls=%fused_computation.20 | loop fusion | flops 8388608 | bytes 12597248 | tf_op jit(solution)/shard_map/sub | solution.py:1262
  499.3 0.6 slice.66
  499.9 0.6 copy.78
  500.5 0.6 fusion.19
  501.1 0.6 slice.65
  501.8 0.6 reduce_sum.59
  502.4 3.2 copy.81
  505.6 1.0 copy.82
  (71 shorter events, 0.4 us)
Async XLA Ops:
  3.5 195.4 %copy-start.15 = (f32[1,1024]{1,0:T(1,128)}, f32[1,1024]{1,0:T(1,128)S(1)}, u32[]{:S(2)}) copy-start(f32[1,1024]{1,0:T(1,128)S(1)} %broadcast_in_dim_reshape.3.skip_ref.refs_19_) | copy-start | bytes 12292
  5.4 193.6 %copy-start.14 = (f32[2,1,1024]{2,1,0:T(1,128)}, f32[2,1,1024]{2,1,0:T(1,128)S(1)}, u32[]{:S(2)}) copy-start(f32[2,1,1024]{2,1,0:T(1,128)S(1)} %broadcast_in_dim.12.segrow_ref.refs_13_) | copy-start | bytes 24580
  16.8 4.7 copy-start.19
  16.8 4.7 copy-start.23
  21.6 177.4 %copy-start.1 = (f32[2,1024,8]{2,1,0:T(8,128)}, f32[2,1024,8]{2,1,0:T(8,128)S(1)}, u32[]{:S(2)}) copy-start(f32[2,1024,8]{2,1,0:T(8,128)S(1)} %stack.69.cols_ref.refs_12_) | copy-start | bytes 196612
  21.6 2.0 copy-start.2
  21.6 2.2 copy-start.10
  21.6 2.3 copy-start.11
  159.9 10.7 %copy-start.6 = (bf16[2048,1024]{1,0:T(8,128)(2,1)}, bf16[2048,1024]{1,0:T(8,128)(2,1)S(1)}, u32[]{:S(2)}) copy-start(bf16[2048,1024]{1,0:T(8,128)(2,1)S(1)} %get-tuple-element.38.wz_hbm) | copy-start | bytes 12582916
  159.9 10.7 %copy-start.9 = (bf16[2048,384]{1,0:T(8,128)(2,1)}, bf16[2048,384]{1,0:T(8,128)(2,1)S(1)}, u32[]{:S(2)}) copy-start(bf16[2048,384]{1,0:T(8,128)(2,1)S(1)} %get-tuple-element.36.wb_hbm) | copy-start | bytes 4718596
  159.9 13.7 %copy-start.4 = (bf16[1024,2048]{1,0:T(8,128)(2,1)}, bf16[1024,2048]{1,0:T(8,128)(2,1)S(1)}, u32[]{:S(2)}) copy-start(bf16[1024,2048]{1,0:T(8,128)(2,1)S(1)} %get-tuple-element.40.refs_4_) | copy-start | bytes 12582916
  159.9 24.9 %copy-start.5 = (bf16[2048,1024]{1,0:T(8,128)(2,1)}, bf16[2048,1024]{1,0:T(8,128)(2,1)S(1)}, u32[]{:S(2)}) copy-start(bf16[2048,1024]{1,0:T(8,128)(2,1)S(1)} %get-tuple-element.35.wx_hbm) | copy-start | bytes 12582916
  159.9 13.7 %slice-start = ((s8[8388608]{0:T(1024)(128)(4,1)}), s8[4194304]{0:T(1024)(128)(4,1)S(1)}, s32[]{:S(2)}) async-start(s8[8388608]{0:T(1024)(128)(4,1)} %bitcast.88), calls=%async_computation | async-start | bytes 8388608
  159.9 13.7 %slice-start.1 = ((s8[8388608]{0:T(1024)(128)(4,1)}), s8[4194304]{0:T(1024)(128)(4,1)S(1)}, s32[]{:S(2)}) async-start(s8[8388608]{0:T(1024)(128)(4,1)} %bitcast.88), calls=%async_computation.1 | async-start | bytes 8388608
  170.9 28.1 %copy-start = (f32[2,1024,16]{2,1,0:T(8,128)}, f32[2,1024,16]{2,1,0:T(8,128)S(1)}, u32[]{:S(2)}) copy-start(f32[2,1024,16]{2,1,0:T(8,128)S(1)} %constant_dynamic-slice_fusion.dt_ref.refs_11_) | copy-start | bytes 393220
  184.8 14.2 %copy-start.12 = (f32[5,1024]{1,0:T(8,128)S(1)}, f32[5,1024]{1,0:T(8,128)}, u32[]{:S(2)}) copy-start(f32[5,1024]{1,0:T(8,128)} %refs_15_.1) | copy-start | bytes 61444
  184.8 14.2 %copy-start.13 = (bf16[16,1024]{1,0:T(8,128)(2,1)S(1)}, bf16[16,1024]{1,0:T(8,128)(2,1)}, u32[]{:S(2)}) copy-start(bf16[16,1024]{1,0:T(8,128)(2,1)} %constant.36.clone.spread_ref.refs_20_) | copy-start | bytes 98308
  184.8 14.2 %copy-start.16 = (f32[5,256]{1,0:T(8,128)S(1)}, f32[5,256]{1,0:T(8,128)}, u32[]{:S(2)}) copy-start(f32[5,256]{1,0:T(8,128)} %refs_16_.1) | copy-start | bytes 15364
  184.8 14.2 %copy-start.17 = (f32[16]{0:T(128)S(1)}, f32[16]{0:T(128)}, u32[]{:S(2)}) copy-start(f32[16]{0:T(128)} %param.20) | copy-start | bytes 196
  184.8 14.2 %copy-start.18 = (f32[16]{0:T(128)S(1)}, f32[16]{0:T(128)}, u32[]{:S(2)}) copy-start(f32[16]{0:T(128)} %param.21) | copy-start | bytes 196
  199.0 25.5 %copy-start.7 = (bf16[2048,1024]{1,0:T(8,128)(2,1)S(1)}, bf16[2048,1024]{1,0:T(8,128)(2,1)}, u32[]{:S(2)}) copy-start(bf16[2048,1024]{1,0:T(8,128)(2,1)} %copy-done.6) | copy-start | bytes 12582916
  199.0 25.5 %copy-start.26 = (f32[1024]{0:T(1024)S(1)}, f32[1024]{0:T(1024)}, u32[]{:S(2)}) copy-start(f32[1024]{0:T(1024)} %param.23) | copy-start | bytes 12292
  224.5 20.3 %copy-start.8 = (f32[2,1024,256]{2,1,0:T(8,128)}, f32[2,1024,256]{2,1,0:T(8,128)S(1)}, u32[]{:S(2)}) copy-start(f32[2,1024,256]{2,1,0:T(8,128)S(1)} %get-tuple-element.42.refs_10_) | copy-start | bytes 6291460
  485.7 3.2 copy-start.22
  485.7 4.1 copy-start.25
  485.7 4.6 copy-start.24
  488.9 5.0 copy-start.3
  489.8 4.1 copy-start.20
  499.3 6.3 %copy-start.21 = (f32[1024,256]{1,0:T(8,128)S(1)}, f32[1024,256]{1,0:T(8,128)}, u32[]{:S(2)}) copy-start(f32[1024,256]{1,0:T(8,128)} %get-tuple-element.152) | copy-start | bytes 3145732
